TPU v7x, 128 devices: a whole 4x4x4 slice. The times are simulated.
128 devices in a mesh: seq: 32 (over z_hi, y, x), head: 4 (over z_lo, core).
Axes of the slice: x: 4, y: 4, z: 4 (z_hi: 2, z_lo: 2; z = z_hi * 2 + z_lo), core: 2. Of those that a mesh axis runs over, the one named last changes fastest.
Arguments:
- tokens: bfloat16 [8192, 2048], P('seq'), may hold values from -6 to 6
- query_weight: bfloat16 [2048, 2048], P('seq', 'head'), may hold values from -0.125 to 0.125
- key_weight: bfloat16 [2048, 1024], P('seq', 'head'), may hold values from -0.125 to 0.125
- value_weight: bfloat16 [2048, 1024], P('seq', 'head'), may hold values from -0.125 to 0.125
- gate_weight: bfloat16 [2048, 2048], P('seq', 'head'), may hold values from -0.125 to 0.125
- out_weight: bfloat16 [2048, 2048], P('head', 'seq'), may hold values from -2 to 2
- norm_gain: bfloat16 [2048], P('seq'), may hold values from 0.5 to 1.5
- query_gain: bfloat16 [128], P('seq'), may hold values from 0.5 to 1.5
- key_gain: bfloat16 [128], P('seq'), may hold values from 0.5 to 1.5
- inner_gate: bfloat16 [2048, 6144], P('seq', 'head'), may hold values from -0.125 to 0.125
- inner_lift: bfloat16 [2048, 6144], P('seq', 'head'), may hold values from -0.125 to 0.125
- inner_down: bfloat16 [6144, 2048], P('head', 'seq'), may hold values from -0.078125 to 0.078125
- inner_gain: bfloat16 [2048], P('seq'), may hold values from 0.5 to 1.5
- out_grad: bfloat16 [8192, 2048], P('seq'), may hold values from -6 to 6
- bucket_len: int32 [2], replicated, may hold values from 2176 to 6016, as said below
- seq_len: int32 [2], replicated, may hold values from 2049 to 6016, as said below
- home_block: int32 [32], replicated, may hold values from 0 to 31, as said below
Outputs:
- result: float32 [8192, 2048], P('seq')
- tokens_grad: float32 [8192, 2048], P('seq')
- query_weight_grad: float32 [2048, 2048], P('seq', 'head')
- key_weight_grad: float32 [2048, 1024], P('seq', 'head')
- value_weight_grad: float32 [2048, 1024], P('seq', 'head')
- gate_weight_grad: float32 [2048, 2048], P('seq', 'head')
- out_weight_grad: float32 [2048, 2048], P('head', 'seq')
- norm_gain_grad: float32 [2048], P('seq')
- query_gain_grad: float32 [128], P('seq')
- key_gain_grad: float32 [128], P('seq')
- inner_gate_grad: float32 [2048, 6144], P('seq', 'head')
- inner_lift_grad: float32 [2048, 6144], P('seq', 'head')
- inner_down_grad: float32 [6144, 2048], P('head', 'seq')
- inner_gain_grad: float32 [2048], P('seq')
Inputs may be any that keep to these rules, and one draw needn't show every extreme that they name: `bucket_len`: the 2 buckets are multiples of 128 and fill the 8192 stream positions end to end. Sequence s fills the first seq_len[s] positions of bucket s; fewer than 128 positions of a bucket are padding. `home_block`: A permutation of the 32 stream blocks.
All inputs are finite; a program needn't handle non-finite values.
Results may differ from a plain program's by a relative error of at most 0.035.
Values may be sent and summed in bfloat16 or wider, within the bound.
No kernel may reach another device: no remote copies, remote signals or barrier semaphores. Data moves between devices by JAX's collectives and lax.ppermute only.
A program may use at most 192 MiB of HBM per device.

v0:
```python
import jax
import jax.numpy as jnp
from jax import lax
from jax.experimental import pallas as pl
from jax.experimental.pallas import tpu as pltpu
from jax.sharding import Mesh
from jax.sharding import PartitionSpec as P

HD = 128
BLOCK = 256
EPS = 1e-06
THETA = 1000000.0
LOG2E = 1.4426950408889634
SCALE = HD ** (-0.5)
PLANE = ("y", "x")
bfloat = jnp.bfloat16
single = jnp.float32


def rms_parts(value):
    factor = lax.rsqrt(jnp.mean(value * value, axis=-1, keepdims=True) + EPS)
    return (value * factor, factor)


def rms_back(grad, unit_val, factor, gain):
    scaled = grad * gain
    return factor * (scaled - unit_val * jnp.mean(unit_val * scaled, axis=-1, keepdims=True))


def swap(value, axis):
    return lax.ppermute(value, axis, [(0, 1), (1, 0)])


def swap_both(value):
    return lax.ppermute(value, ("zh", "zl"), [(0, 3), (1, 2), (2, 1), (3, 0)])


def line_sum(near, far):
    return line_sum_end(line_sum_middle(near, far))


def line_sum_middle(near, far):
    return near + swap(far.astype(bfloat), "c").astype(single)


def line_sum_end(here, beside=None):
    made = None
    if beside is not None:
        here, needs = lax.optimization_barrier((here, beside[1]))
        made = beside[0](needs)
    sent = here.astype(bfloat)
    got = (swap(sent[64:128], "zl"), swap(sent[128:192], "zh"), swap_both(sent[192:256]))
    if beside is not None:
        got, made = lax.optimization_barrier((got, made))
    one, two, three = (piece.astype(single) for piece in got)
    total = (here[:64] + one) + (two + three)
    return total if beside is None else (total, made)


def shift(value, axis, step):
    return lax.ppermute(value, axis, [(i, (i + step) % 4) for i in range(4)])


def plane_gather(one, two, later, ring):
    got = [
        [shift(value, axis, -step) for step in range(1, 4)]
        for value, axis in ((one, "x"), (two, "y"))
    ]
    got, later = lax.optimization_barrier((got, later))
    lines = [jnp.stack([v] + parts, axis=0) for v, parts in zip((one, two), got)]
    if not ring:
        pieces = [
            [line] + [shift(line, axis, -step) for step in range(1, 4)]
            for line, axis in zip(lines, ("y", "x"))
        ]
        return pieces, later
    next_to = [(shift(line, axis, -1), shift(line, axis, 1)) for line, axis in zip(lines, ("y", "x"))]
    next_to = lax.optimization_barrier(next_to)
    return [
        [line, up, shift(up[:2], axis, -1), shift(down[2:], axis, 1), down]
        for line, (up, down), axis in zip(lines, next_to, ("y", "x"))
    ], later


def add_halves(groups):
    def kernel(*refs):
        for number in range(len(groups)):
            one, up, four, down = refs[4 * number : 4 * number + 4]
            first, second = refs[4 * len(groups) + 2 * number : 4 * len(groups) + 2 * number + 2]
            first[0:2] = (one[0:2].astype(single) + up[...].astype(single)).astype(bfloat)
            first[2:4] = one[2:4]
            second[0:2] = four[0:2]
            second[2:4] = (four[2:4].astype(single) + down[...].astype(single)).astype(bfloat)

    outs = pl.pallas_call(
        kernel,
        out_shape=[
            shaped(bfloat, *one.shape) for one, _, _, _ in groups for _ in range(2)
        ],
        in_specs=[VMEM] * (4 * len(groups)),
        out_specs=[VMEM] * (2 * len(groups)),
        compiler_params=pltpu.CompilerParams(vmem_limit_bytes=8 * 2**20),
        cost_estimate=pl.CostEstimate(flops=2**20, bytes_accessed=5 * 2**20, transcendentals=0),
        name="add_halves",
    )(*(part for group in groups for part in group))
    return [tuple(outs[2 * i : 2 * i + 2]) for i in range(len(groups))]


def plane_sum(one, two, first, second):
    both = list(zip((one, two), ("x", "y")))
    across = [(shift(v[2], axis, 1), shift(v[3], axis, -1)) for v, axis in both]
    across, first = lax.optimization_barrier((across, first))
    sent = add_halves([(v[1], up, v[4], down) for (v, _), (up, down) in zip(both, across)])
    got = [(shift(up, axis, 1), shift(down, axis, -1)) for (_, axis), (up, down) in zip(both, sent)]
    got = lax.optimization_barrier(got)
    sums = [
        v[0].astype(single) + (up.astype(single) + down.astype(single))
        for (v, _), (up, down) in zip(both, got)
    ]
    got = [
        [shift(v[step].astype(bfloat), axis, step) for step in range(1, 4)]
        for v, axis in zip(sums, ("y", "x"))
    ]
    got, second = lax.optimization_barrier((got, second))
    sums = [
        (v[0] + parts[0].astype(single)) + (parts[1].astype(single) + parts[2].astype(single))
        for v, parts in zip(sums, got)
    ]
    return sums[0], sums[1], first, second


def line_gather(own):
    near = jnp.concatenate([own, swap(own, "zl"), swap(own, "zh"), swap_both(own)], axis=0)
    return jnp.concatenate([near, swap(near, "c")], axis=0)


def head_sum(value):
    across = lax.ppermute(value, ("zl", "c"), [(0, 3), (1, 2), (2, 1), (3, 0)])
    return (value + swap(value, "c")) + (swap(value, "zl") + across)


def head_gather(own, mine, later=None):
    near = jnp.concatenate([own, swap(own, "zl")], axis=0)
    if later is not None:
        near, later = lax.optimization_barrier((near, later))
    parts = jnp.concatenate([near, swap(near, "c")], axis=0).reshape(4, 64, -1)
    rows = []
    for place in range(4):
        other = place ^ mine
        slot = (other & 1) * 2 + (other >> 1)
        rows.append(lax.dynamic_index_in_dim(parts, slot, 0, keepdims=False))
    rows = jnp.concatenate(rows, axis=0).astype(single)
    return rows if later is None else (rows, later)


def row_place(index, zl, c):
    core = (index >> 7) & 1
    low = (index >> 6) & 1
    return ((low ^ zl) * 2 + (core ^ c)) * 64 + (index & 63)


def block_range(block, cut, ends):
    first = block * BLOCK
    last = first + BLOCK - 1
    low_least = jnp.where(first >= cut, cut, 0)
    low_most = jnp.where(last >= cut, cut, 0)
    high_least = jnp.minimum(first, jnp.where(first >= cut, ends[1], ends[0]))
    start = low_least // BLOCK
    whole = jnp.minimum((low_most + BLOCK - 1) // BLOCK, block + 1)
    whole_end = jnp.maximum((high_least + 1) // BLOCK, whole)
    return start, whole, whole_end, block + 1


def stacked(ref, half):
    near = half * 128
    return jnp.concatenate(
        [
            ref[near : near + 128, 0:HD],
            ref[256 + near : 384 + near, 0:HD],
            ref[near : near + 128, HD : 2 * HD],
            ref[256 + near : 384 + near, HD : 2 * HD],
        ],
        axis=0,
    )


def unstack(ref, half, value):
    near = half * 128
    ref[near : near + 128, 0:HD] = value[0:128]
    ref[256 + near : 384 + near, 0:HD] = value[128:256]
    ref[near : near + 128, HD : 2 * HD] = value[256:384]
    ref[256 + near : 384 + near, HD : 2 * HD] = value[384:512]


def key_rows(ref, one, two, half):
    near = pl.multiple_of(half * 128, 128)
    far = pl.multiple_of(256 + half * 128, 128)
    return jnp.concatenate(
        [ref[one, two, pl.ds(near, 128), :], ref[one, two, pl.ds(far, 128), :]], axis=0
    )


def find_slot(info, where, block):
    slot = where[block]
    down = ((slot >> 2) - info[8]) & 3
    across = (slot - info[9]) & 3
    return down, across, (slot >> 4) ^ info[4]


def bring(pairs, sems):
    copies = [pltpu.make_async_copy(*pair, sems.at[i]) for i, pair in enumerate(pairs)]
    for copy in copies:
        copy.start()
    return copies


def ring_targets(buffer):
    return [
        buffer.at[0],
        buffer.at[1],
        buffer.at[2, pl.ds(0, 2)],
        buffer.at[2, pl.ds(2, 2)],
        buffer.at[3],
    ]


def in_hbm(values):
    return [pltpu.with_memory_space_constraint(value, pltpu.HBM) for value in values]


def turned(value, cosine, sine):
    return value * cosine + pltpu.roll(value, HD // 2, 1) * sine


def unit_of(value):
    factor = lax.rsqrt(jnp.mean(value * value, axis=-1, keepdims=True) + EPS)
    return value * factor, factor


def dot_nt(left, right):
    return lax.dot_general(left, right, (((1,), (1,)), ((), ())), preferred_element_type=single)


def dot_tn(left, right):
    return lax.dot_general(left, right, (((0,), (0,)), ((), ())), preferred_element_type=single)


def find_blocks(home, where):
    for slot in range(32):
        where[home[slot]] = slot


def tile_limits(info, half):
    zl, c, cut = info[2], info[3], info[5]
    ends = (info[6] - 1, cut + info[7] - 1)
    block = info[half]
    place = block * BLOCK + row_place(lax.broadcasted_iota(jnp.int32, (1, 512), 1), zl, c)
    second = place >= cut
    low = jnp.where(second, cut, 0)
    high = jnp.minimum(place, jnp.where(second, ends[1], ends[0]))
    return low, high, block_range(block, cut, ends)


def over_blocks(limits, step):
    start, whole, whole_end, stop = limits
    many = (whole_end - whole) // 4
    lax.fori_loop(start, whole, lambda block, _: step(block, 1, True), None)
    lax.fori_loop(0, many, lambda i, _: step(whole + 4 * i, 4, False), None)
    lax.fori_loop(whole + 4 * many, whole_end, lambda block, _: step(block, 1, False), None)
    lax.fori_loop(whole_end, stop, lambda block, _: step(block, 1, True), None)


def together(parts):
    return parts[0] if len(parts) == 1 else jnp.concatenate(parts, axis=0)


def attend_kernel(info, home, *refs):
    ins, (out, logs) = refs[:11], refs[11:13]
    query, keys, values, where, accum, total, sems = refs[13:]
    copies = bring(
        list(zip(ins, [query] + ring_targets(keys) + ring_targets(values))), sems
    )
    find_blocks(home, where)
    for copy in copies:
        copy.wait()
    key_place = row_place(lax.broadcasted_iota(jnp.int32, (256, 512), 0), info[2], info[3])
    for half in range(2):
        low, high, limits = tile_limits(info, half)
        rows = stacked(query, half)
        accum[...] = jnp.zeros_like(accum)
        total[...] = jnp.zeros_like(total)

        def step(block, count, masked):
            slots = [find_slot(info, where, block + i) for i in range(count)]
            key = together([key_rows(keys, down, across, side) for down, across, side in slots])
            value = together([key_rows(values, across, down, side) for down, across, side in slots])
            weight = jnp.exp2(dot_nt(key, rows) * (SCALE * LOG2E))
            if masked:
                place = key_place + block * BLOCK
                weight = jnp.where((place >= low) & (place <= high), weight, 0.0)
            total[...] += jnp.sum(weight.reshape(-1, 8, 512), axis=0)
            accum[...] += dot_tn(value, weight.astype(bfloat))

        over_blocks(limits, step)
        weights = jnp.sum(total[...], axis=0, keepdims=True)
        logs[half] = jnp.log2(weights)
        unstack(out, half, jnp.transpose(accum[...] / weights))


def attend_back_kernel(info, home, logs, gains, *refs):
    ins, (d_pre, gain_grad) = refs[:16], refs[16:18]
    d_keys, d_values = refs[18:23], refs[23:28]
    query, d_out, out, pre, cosine, sine, keys, values = refs[28:36]
    where, key_sum, value_sum, d_rows, d_query, sems = refs[36:]
    targets = [query, d_out, out, pre, cosine, sine] + ring_targets(keys) + ring_targets(values)
    copies = bring(list(zip(ins, targets)), sems)
    find_blocks(home, where)
    key_place = row_place(lax.broadcasted_iota(jnp.int32, (256, 512), 0), info[2], info[3])

    def clear(index, _):
        for accum in (key_sum, value_sum):
            accum[index] = jnp.zeros(accum.shape[1:], single)

    lax.fori_loop(0, 16, clear, None)
    for copy in copies:
        copy.wait()
    for half in range(2):
        low, high, limits = tile_limits(info, half)
        rows = stacked(query, half)
        grads = stacked(d_out, half)
        delta = jnp.sum(
            jnp.transpose(grads.astype(single) * stacked(out, half)), axis=0, keepdims=True
        )
        log = logs[half]
        d_rows[...] = jnp.zeros_like(d_rows)

        def step(block, count, masked):
            slots = [find_slot(info, where, block + i) for i in range(count)]
            key = together([key_rows(keys, down, across, side) for down, across, side in slots])
            value = together([key_rows(values, across, down, side) for down, across, side in slots])
            prob = jnp.exp2(dot_nt(key, rows) * (SCALE * LOG2E) - log)
            if masked:
                place = key_place + block * BLOCK
                prob = jnp.where((place >= low) & (place <= high), prob, 0.0)
            d_score = (prob * (dot_nt(value, grads) - delta)).astype(bfloat)
            d_value = jnp.dot(prob.astype(bfloat), grads, preferred_element_type=single)
            d_key = jnp.dot(d_score, rows, preferred_element_type=single)
            d_rows[...] += dot_tn(key, d_score)
            for i, (down, across, side) in enumerate(slots):
                near = pl.multiple_of(side * 128, 128)
                far = pl.multiple_of(256 + side * 128, 128)
                for accum, slot, grad in (
                    (key_sum, across * 4 + down, d_key),
                    (value_sum, down * 4 + across, d_value),
                ):
                    accum[slot, pl.ds(near, 128), :] += grad[i * 256 : i * 256 + 128]
                    accum[slot, pl.ds(far, 128), :] += grad[i * 256 + 128 : i * 256 + 256]

        over_blocks(limits, step)
        unstack(d_query, half, jnp.transpose(d_rows[...]) * SCALE)
    for one in range(4):
        for two in range(4):
            number, place = (one, two) if one < 2 else (4, two) if one == 3 else (2 + two // 2, two % 2)
            d_keys[number][place] = (key_sum[one * 4 + two] * SCALE).astype(bfloat)
            d_values[number][place] = value_sum[one * 4 + two].astype(bfloat)
    gain = gains[0:1]
    total = jnp.zeros((1, HD), single)
    for head in range(2):
        columns = slice(head * HD, (head + 1) * HD)
        d_turned = turned(d_query[:, columns], cosine[...], -sine[...])
        unit, factor = unit_of(pre[:, columns])
        total += jnp.sum(d_turned * unit, axis=0, keepdims=True)
        d_pre[:, columns] = rms_back(d_turned, unit, factor, gain).astype(bfloat)
    gain_grad[...] = total


def line_order(info):
    for core in range(2):
        for source in range(2):
            for low in range(2):
                there = ((low ^ info[2]) * 2 + (core ^ info[3])) * 64
                yield core * 4 + source * 2 + low, source, pl.multiple_of(there, 64)


def arrange_kernel(info, own, other, out):
    for place, source, there in line_order(info):
        out[place * 64 : place * 64 + 64, :] = (own, other)[source][pl.ds(there, 64), :]


def project_pairs_kernel(info, cosine, sine, *refs):
    normed, key, value, pre, weights, gains, small, extra, came, own, other, sems = refs[10:]
    copies = bring(list(zip(refs[:10], [own, other] + [came.at[i] for i in range(8)])), sems)
    for copy in copies:
        copy.wait()
    for one in range(4):
        for two in range(4):
            for number, y, x, column in ((one, one, two, 0), (4 + one, two, one, HD)):
                plane = ((y + info[8]) & 3) * 4 + ((x + info[9]) & 3)
                for side in range(2):
                    to = pl.ds(pl.multiple_of(side * 1024 + plane * 64, 64), 64)
                    block = came[number, two, side * 64 : side * 64 + 64, :]
                    weights[to, column : column + HD] = block[:, :HD]
                    extra[to, column : column + HD] = block[:, HD:]
    gains[...] = jnp.transpose(extra[:, 0:HD].astype(single))[0:8]
    total = jnp.zeros((16, HD), single)
    for block in range(32):
        total += extra[block * 64 : block * 64 + 16, HD : 2 * HD].astype(single)
    small[...] = total[0:8]
    gain = gains[0:1]
    for place, source, there in line_order(info):
        unit, _ = unit_of((own, other)[source][pl.ds(there, 64), :].astype(single))
        normed[place * 64 : place * 64 + 64, :] = (unit * gain).astype(bfloat)
    both = jnp.dot(normed[...], weights[...], preferred_element_type=single)
    pre[...] = both[:, :HD]
    unit, _ = unit_of(both[:, :HD])
    key[...] = turned(unit * small[1:2], cosine[...], sine[...]).astype(bfloat)
    value[...] = both[:, HD:].astype(bfloat)


def project_query_kernel(normed, weights, cosine, sine, gains, query, pre, gate_act):
    both = jnp.dot(normed[...], weights[:, 0 : 4 * HD], preferred_element_type=single)
    for head in range(2):
        columns = slice(head * HD, (head + 1) * HD)
        pre[:, columns] = both[:, columns]
        unit, _ = unit_of(both[:, columns])
        query[:, columns] = turned(unit * gains[0:1], cosine[...], sine[...]).astype(bfloat)
    gate_act[...] = jax.nn.sigmoid(both[:, 2 * HD : 4 * HD])


VMEM = pl.BlockSpec(memory_space=pltpu.VMEM)
SMEM = pl.BlockSpec(memory_space=pltpu.SMEM)
ANY = pl.BlockSpec(memory_space=pl.ANY)
HBM = pl.BlockSpec(memory_space=pltpu.HBM)


def shaped(dtype, *shape):
    return jax.ShapeDtypeStruct(shape, dtype)


def arrange(info, own, other):
    return pl.pallas_call(
        arrange_kernel,
        out_shape=shaped(own.dtype, 512, own.shape[1]),
        in_specs=[SMEM, VMEM, VMEM],
        out_specs=VMEM,
        cost_estimate=pl.CostEstimate(flops=0, bytes_accessed=4 * 2**20, transcendentals=0),
        name="arrange",
    )(info, own, other)


def project_pairs(info, own, other, cosine, sine, pieces):
    width = own.shape[1]
    return pl.pallas_call(
        project_pairs_kernel,
        out_shape=(
            shaped(bfloat, 512, width),
            shaped(bfloat, 512, HD),
            shaped(bfloat, 512, HD),
            shaped(single, 512, HD),
            shaped(bfloat, width, 2 * HD),
            shaped(single, 8, width),
            shaped(single, 8, HD),
        ),
        in_specs=[SMEM] + [VMEM] * 2 + [HBM] * 10,
        out_specs=[VMEM] * 7,
        scratch_shapes=[
            pltpu.VMEM((width, 2 * HD), bfloat),
            pltpu.VMEM((8, 4, HD, 2 * HD), bfloat),
            pltpu.VMEM((BLOCK, width), bfloat),
            pltpu.VMEM((BLOCK, width), bfloat),
            pltpu.SemaphoreType.DMA((10,)),
        ],
        compiler_params=pltpu.CompilerParams(vmem_limit_bytes=16 * 2**20),
        cost_estimate=pl.CostEstimate(
            flops=2**30, bytes_accessed=8 * 2**20, transcendentals=2**10
        ),
        name="project_pairs",
    )(info, cosine, sine, *in_hbm([own, other, *pieces[0], *pieces[1]]))


def project_query(normed, weights, cosine, sine, gains):
    return pl.pallas_call(
        project_query_kernel,
        out_shape=(
            shaped(bfloat, 512, 2 * HD),
            shaped(single, 512, 2 * HD),
            shaped(single, 512, 2 * HD),
        ),
        in_specs=[VMEM] * 5,
        out_specs=[VMEM] * 3,
        compiler_params=pltpu.CompilerParams(vmem_limit_bytes=12 * 2**20),
        cost_estimate=pl.CostEstimate(
            flops=2**30, bytes_accessed=8 * 2**20, transcendentals=2**17
        ),
        name="project_query",
    )(normed, weights, cosine, sine, gains)


def attend(info, home, query, pieces):
    return pl.pallas_call(
        attend_kernel,
        out_shape=(shaped(single, 512, 2 * HD), shaped(single, 2, 1, 512)),
        in_specs=[SMEM, SMEM] + [HBM] * 11,
        out_specs=(VMEM, VMEM),
        scratch_shapes=[
            pltpu.VMEM((512, 2 * HD), bfloat),
            pltpu.VMEM((4, 4, 512, HD), bfloat),
            pltpu.VMEM((4, 4, 512, HD), bfloat),
            pltpu.SMEM((32,), jnp.int32),
            pltpu.VMEM((HD, 512), single),
            pltpu.VMEM((8, 512), single),
            pltpu.SemaphoreType.DMA((11,)),
        ],
        compiler_params=pltpu.CompilerParams(vmem_limit_bytes=12 * 2**20),
        cost_estimate=pl.CostEstimate(
            flops=4 * 2**30, bytes_accessed=6 * 2**20, transcendentals=4 * 2**20
        ),
        name="attend",
    )(info, home, *in_hbm([query, *pieces[0], *pieces[1]]))


def attend_back(info, home, query, d_out, out, logs, pre, cosine, sine, gains, pieces):
    outs = pl.pallas_call(
        attend_back_kernel,
        out_shape=[shaped(bfloat, 512, 2 * HD), shaped(single, 1, HD)]
        + [pltpu.HBM((count, 512, HD), bfloat) for count in (4, 4, 2, 2, 4)] * 2,
        in_specs=[SMEM, SMEM, VMEM, VMEM] + [HBM] * 16,
        out_specs=[VMEM] * 12,
        scratch_shapes=[
            pltpu.VMEM((512, 2 * HD), bfloat),
            pltpu.VMEM((512, 2 * HD), bfloat),
            pltpu.VMEM((512, 2 * HD), single),
            pltpu.VMEM((512, 2 * HD), single),
            pltpu.VMEM((512, HD), single),
            pltpu.VMEM((512, HD), single),
            pltpu.VMEM((4, 4, 512, HD), bfloat),
            pltpu.VMEM((4, 4, 512, HD), bfloat),
            pltpu.SMEM((32,), jnp.int32),
            pltpu.VMEM((16, 512, HD), single),
            pltpu.VMEM((16, 512, HD), single),
            pltpu.VMEM((HD, 512), single),
            pltpu.VMEM((512, 2 * HD), single),
            pltpu.SemaphoreType.DMA((16,)),
        ],
        compiler_params=pltpu.CompilerParams(vmem_limit_bytes=28 * 2**20),
        cost_estimate=pl.CostEstimate(
            flops=10 * 2**30, bytes_accessed=12 * 2**20, transcendentals=4 * 2**20
        ),
        name="attend_back",
    )(
        info,
        home,
        logs,
        gains,
        *in_hbm([query, d_out, out, pre, cosine, sine, *pieces[0], *pieces[1]]),
    )
    return outs[0], outs[1], outs[2:7], outs[7:12]


def plane_grads(lefts, rights, tile, rows=128, columns=None, into=None, extras=(), by_x=False):
    starts = []
    count = 0
    for _, right in rights:
        starts.append(count)
        count += right.shape[1] // tile
    spans = list(zip(starts, starts[1:] + [count]))
    depth, height = lefts[0].shape
    columns = columns or count * tile
    shift_by = 0 if into is None else columns // tile - count
    flips = {}
    for (number, _), start in zip(rights, starts):
        flips.setdefault(number, start)

    def kernel(*refs):
        left_refs, right_refs = refs[: len(lefts)], refs[len(lefts) : len(lefts) + len(rights)]
        extra_refs = refs[len(lefts) + len(rights) : len(lefts) + len(rights) + len(extras)]
        out, flipped = refs[-2:]
        step = pl.program_id(0)

        def flip(left):
            for group in range(8):
                side, y = group // 4, group % 4
                turned = jnp.transpose(left[:, group * 256 : group * 256 + 256])
                for x in range(4):
                    first = ((x * 4 + y if by_x else y * 4 + x) * 2 + side) * 64
                    flipped[first : first + 64, :] = turned[x * 64 : x * 64 + 64]

        def product(right):
            for one in range(4):
                left = flipped[one * 512 : one * 512 + 512, :]
                part = jnp.dot(left, right, preferred_element_type=single).astype(bfloat)
                out[one * 4 : one * 4 + 4, 0:128] = part.reshape(4, 128, tile)
            for number, ref in enumerate(extra_refs):
                out[:, 128:144, number * HD : (number + 1) * HD] = jnp.broadcast_to(
                    ref[...].astype(bfloat)[None], (16, 16, HD)
                )

        for number, start in flips.items():
            pl.when(step == start)(lambda number=number: flip(left_refs[number]))
        for ref, (start, stop) in zip(right_refs, spans):
            pl.when((step >= start) & (step < stop))(lambda ref=ref: product(ref[...]))

    def right_spec(start, stop):
        return pl.BlockSpec(
            (depth, tile), lambda i: (0, jnp.minimum(jnp.maximum(i - start, 0), stop - start - 1))
        )

    return pl.pallas_call(
        kernel,
        grid=(count,),
        in_specs=[
            pl.BlockSpec((depth, height), lambda i: (0, 0), pipeline_mode=pl.Buffered(1))
            for _ in lefts
        ]
        + [right_spec(*span) for span in spans]
        + [pl.BlockSpec((1, HD), lambda i: (0, 0)) for _ in extras]
        + ([] if into is None else [ANY]),
        out_specs=pl.BlockSpec((16, rows, tile), lambda i: (0, 0, i + shift_by)),
        out_shape=pltpu.HBM((16, rows, columns), bfloat),
        input_output_aliases={} if into is None else {len(lefts) + len(rights) + len(extras): 0},
        scratch_shapes=[pltpu.VMEM((height, depth), bfloat)],
        compiler_params=pltpu.CompilerParams(
            vmem_limit_bytes=18 * 2**20, dimension_semantics=("arbitrary",)
        ),
        cost_estimate=pl.CostEstimate(
            flops=2 * depth * height * count * tile,
            bytes_accessed=2 * (depth + height) * count * tile + 2 * depth * height,
            transcendentals=0,
        ),
        name="plane_grads",
    )(*lefts, *(right for _, right in rights), *extras, *([] if into is None else [into]))


def columns_of(weight, side, width):
    return lax.dynamic_slice_in_dim(weight, side * width, width, 1)


def rows_of(weight, side, width):
    return lax.dynamic_slice_in_dim(weight, side * width, width, 0)


def in_order(zh, own, other, axis):
    first = jnp.where(zh == 0, own, other)
    second = jnp.where(zh == 0, other, own)
    return jnp.concatenate([first, second], axis=axis)


def gather_plane(block):
    whole = lax.all_gather(block, PLANE, axis=1, tiled=True)
    return whole.reshape(-1, block.shape[-1])


def per_device(
    tokens,
    query_weight,
    key_weight,
    value_weight,
    gate_weight,
    out_weight,
    norm_gain,
    query_gain,
    key_gain,
    inner_gate,
    inner_lift,
    inner_down,
    inner_gain,
    out_grad,
    bucket_len,
    seq_len,
    home_block,
):
    zh = lax.axis_index("zh")
    zl = lax.axis_index("zl")
    c = lax.axis_index("c")
    mine = zl * 2 + c
    width = tokens.shape[1]
    seq_index = zh * 16 + lax.axis_index("y") * 4 + lax.axis_index("x")
    block_own = lax.dynamic_index_in_dim(home_block, seq_index, 0, keepdims=False)
    block_other = lax.dynamic_index_in_dim(home_block, seq_index ^ 16, 0, keepdims=False)
    info = jnp.stack(
        [
            block_own,
            block_other,
            zl,
            c,
            zh,
            bucket_len[0],
            seq_len[0],
            seq_len[1],
            lax.axis_index("y"),
            lax.axis_index("x"),
        ]
    ).astype(jnp.int32)

    lane = jnp.arange(HD, dtype=jnp.int32)

    def head_gain(vector):
        return jnp.where(lane // 4 == seq_index, jnp.tile(vector, 32), 0)

    norm_columns = jnp.pad(jnp.stack([norm_gain, inner_gain], axis=1), ((0, 0), (0, HD - 2)))
    head_rows = jnp.pad(
        jnp.stack([head_gain(query_gain), head_gain(key_gain)], axis=0), ((0, 62), (0, 0))
    ).astype(bfloat)

    def pairs_pack(side):
        return jnp.concatenate(
            [
                columns_of(key_weight, side, HD),
                norm_columns,
                columns_of(value_weight, side, HD),
                head_rows,
            ],
            axis=1,
        )

    def outer_pack(side):
        return jnp.concatenate(
            [
                columns_of(query_weight, side, 256),
                columns_of(gate_weight, side, 256),
                rows_of(out_weight, side, 256).T,
            ],
            axis=1,
        )

    def inner_pack(side):
        gate, lift, down = inner_shards
        return jnp.concatenate(
            [columns_of(gate, side, 768), columns_of(lift, side, 768), rows_of(down, side, 768).T],
            axis=1,
        )

    def pair_up(pack):
        own = pack(zh)
        other = swap(pack(1 - zh), "zh")
        return in_order(zh, own[None], other[None], 0)

    first_block = pair_up(
        lambda side: jnp.concatenate([pairs_pack(side), outer_pack(side)], axis=1)
    )
    index = jnp.arange(512, dtype=jnp.int32)
    half_of = (index >> 7) & 1
    place = jnp.where(half_of == 0, block_own, block_other) * BLOCK + row_place(
        ((index >> 8) << 7) | (index & 127), zl, c
    )
    offset = jnp.where(place >= bucket_len[0], place - bucket_len[0], place)
    freq = jnp.power(THETA, -jnp.arange(HD // 2, dtype=single) * 2.0 / HD)
    angle = offset.astype(single)[:, None] * freq[None, :]
    cosine = jnp.cos(angle)
    sine = jnp.sin(angle)
    cosine = jnp.concatenate([cosine, cosine], axis=1)
    sine = jnp.concatenate([-sine, sine], axis=1)

    first_block, cosine, sine, info = lax.optimization_barrier((first_block, cosine, sine, info))
    tokens_other = swap(tokens, "zh")
    pairs_block, outer_block = first_block[:, :, : 4 * HD], first_block[:, :, 4 * HD :]
    outer = gather_plane(outer_block)
    pairs_wide = pairs_block.reshape(HD, 4 * HD)
    weight_pieces, _ = plane_gather(pairs_wide[:, : 2 * HD], pairs_wide[:, 2 * HD :], (), False)
    normed, key_rot, value, k_pre, w_pairs, gains, head_gains = project_pairs(
        info, tokens, tokens_other, cosine, sine, weight_pieces
    )
    key_rot, inner_shards = lax.optimization_barrier(
        (key_rot, (inner_gate, inner_lift, inner_down))
    )
    inner_block = pair_up(inner_pack)
    gain_norm, gain_inner = gains[0:1], gains[1:2]
    gain_query, gain_key = head_gains[0:1], head_gains[1:2]
    w_heads = outer[:, :512]
    w_out = outer[:, 512:]
    query, q_pre, gate_sig = project_query(normed, outer, cosine, sine, head_gains)
    pieces, (inner_block, out_grad_sent) = plane_gather(
        key_rot, value, (inner_block, out_grad), True
    )
    rows_grad = arrange(info, out_grad, swap(out_grad_sent, "zh"))
    inner = gather_plane(inner_block)
    w_gate_lift = inner[:, :1536]
    w_down = inner[:, 1536:]
    query, rows_grad = lax.optimization_barrier((query, rows_grad))
    attended, logs = attend(info, home_block, query, pieces)
    gated = (attended * gate_sig).astype(bfloat)

    def line_product(left, right):
        return line_sum(dot_nt(left[:256], right), dot_nt(left[256:], right))

    inputs = rows_of(tokens, mine, 64).astype(single)
    mixed_in = inputs + line_product(gated, w_out)
    unit_two, factor_two = rms_parts(mixed_in)
    normed_two = line_gather((unit_two * gain_inner).astype(bfloat))
    d_hidden = jnp.dot(rows_grad, w_down, preferred_element_type=single)
    gate_lift = jnp.dot(normed_two, w_gate_lift, preferred_element_type=single)
    gate_val = gate_lift[:, :768]
    lift_val = gate_lift[:, 768:]
    gate_act = jax.nn.sigmoid(gate_val)
    hidden = (gate_val * gate_act * lift_val).astype(bfloat)
    d_gate = (d_hidden * lift_val * gate_act * (1.0 + gate_val * (1.0 - gate_act))).astype(bfloat)
    d_lift = (d_hidden * gate_val * gate_act).astype(bfloat)
    d_gate_lift = jnp.concatenate([d_gate, d_lift], axis=1)

    def inner_grads(needs):
        return plane_grads(
            [normed_two, rows_grad],
            [(0, needs[0]), (0, needs[1]), (1, needs[2])],
            384,
        )

    d_normed_two, grad_inner = line_sum_end(
        line_sum_middle(dot_nt(d_gate_lift[:256], w_gate_lift), dot_nt(d_gate_lift[256:], w_gate_lift)),
        (inner_grads, (d_gate, d_lift, hidden)),
    )

    def scatter_plane(grad):
        part = lax.psum_scatter(grad, PLANE, scatter_dimension=0, tiled=False)
        return part.reshape(2, 64, -1)

    part = scatter_plane(grad_inner)
    d_mixed = rows_grad[:64].astype(single) + rms_back(
        d_normed_two, unit_two, factor_two, gain_inner
    )
    d_attn = line_gather(d_mixed.astype(bfloat))
    d_gated = jnp.dot(d_attn, w_out, preferred_element_type=single)
    d_attended = (d_gated * gate_sig).astype(bfloat)
    d_gate_pre = (d_gated * attended * gate_sig * (1.0 - gate_sig)).astype(bfloat)

    def rounded(rows):
        return lax.reduce_precision(rows, 8, 7).astype(bfloat)

    def both_sides(part):
        own = lax.dynamic_index_in_dim(part, zh, 0, keepdims=False).astype(single)
        sent = lax.dynamic_index_in_dim(part, 1 - zh, 0, keepdims=False).astype(bfloat)
        sent, part = lax.optimization_barrier((sent, part))
        return own, swap(sent, "zh").astype(single), part

    d_q_pre, query_gain_part, d_keys, d_values = attend_back(
        info,
        home_block,
        query,
        d_attended,
        attended,
        logs,
        q_pre,
        cosine,
        sine,
        head_gains,
        pieces,
    )
    grad_outer = plane_grads(
        [d_attn, normed], [(0, gated), (1, d_gate_pre), (1, d_q_pre)], 256, by_x=True
    )
    d_heads = jnp.concatenate([d_q_pre, d_gate_pre], axis=1)

    d_key, d_value, grad_outer, (normed_near, normed_far) = plane_sum(
        d_keys,
        d_values,
        grad_outer,
        (dot_nt(d_heads[:256], w_heads), dot_nt(d_heads[256:], w_heads)),
    )
    grad_outer, part = lax.optimization_barrier((grad_outer, part))
    rest = lax.psum_scatter(
        grad_outer.reshape(4, 4, 128, -1), "x", scatter_dimension=0, tiled=False
    )
    rest = lax.psum_scatter(rest, "y", scatter_dimension=0, tiled=False).reshape(2, 64, -1)
    k_unit, k_factor = rms_parts(k_pre)
    d_k_turned = d_key * cosine - jnp.roll(d_key, HD // 2, axis=1) * sine
    key_gain_part = jnp.sum(d_k_turned * k_unit, axis=0, keepdims=True)
    d_k_pre = rms_back(d_k_turned, k_unit, k_factor, gain_key).astype(bfloat)
    d_kv_pre = jnp.concatenate([d_k_pre, d_value.astype(bfloat)], axis=1)
    normed_far = (normed_far + dot_nt(d_kv_pre[256:], w_pairs)).astype(bfloat)
    normed_far, d_kv_pre = lax.optimization_barrier((normed_far, d_kv_pre))
    pairs_sent = plane_grads(
        [normed], [(0, d_kv_pre)], 256, rows=144, extras=(query_gain_part, key_gain_part)
    )
    pairs_sent, d_kv_pre = lax.optimization_barrier((pairs_sent, d_kv_pre))
    normed_near = normed_near + dot_nt(d_kv_pre[:256], w_pairs)
    pairs_got = lax.all_to_all(pairs_sent, PLANE, 0, 0, tiled=True)
    here, hidden = lax.optimization_barrier((line_sum_middle(normed_near, normed_far), hidden))
    d_normed = line_sum_end(here)
    result_rows = mixed_in + line_product(hidden, w_down)
    unit_in, factor_in = rms_parts(inputs)
    token_rows = d_mixed + rms_back(d_normed, unit_in, factor_in, gain_norm)

    part_own, part_got, part = both_sides(part)
    pairs_got, rest, token_rows, part_got = lax.optimization_barrier(
        (pairs_got, rest, token_rows, part_got)
    )
    pairs_sum = jnp.sum(pairs_got.astype(single), axis=0)
    result, (pairs_sum, part) = head_gather(rounded(result_rows), mine, (pairs_sum, part))
    gain_part = pairs_sum[128]
    pair_part = pairs_sum[:128].reshape(2, 64, 256)
    tokens_grad = head_gather(rounded(token_rows), mine)

    def weighted(block, part):
        return jnp.sum(block.astype(single) * part.astype(single), axis=2)

    norm_part = (
        weighted(outer_block[:, :, :256], rest[:, :, 512:])
        + weighted(outer_block[:, :, 256:512], rest[:, :, 256:512])
        + weighted(pairs_block[:, :, :HD], pair_part[:, :, :HD])
        + weighted(pairs_block[:, :, 2 * HD : 3 * HD], pair_part[:, :, HD:])
    ) / pairs_block[:, :, HD].astype(single)
    inner_gain_part = weighted(inner_block[:, :, :1536], part[:, :, :1536]) / pairs_block[
        :, :, HD + 1
    ].astype(single)
    gain_line = jnp.concatenate(
        [
            norm_part.reshape(HD),
            inner_gain_part.reshape(HD),
            gain_part,
        ]
    ).reshape(4, HD)
    gain_line = lax.reduce_precision(gain_line, 8, 7)
    last = jnp.concatenate([rest.astype(single), pair_part], axis=2)
    last_own = lax.dynamic_index_in_dim(last, zh, 0, keepdims=False)
    last_sent = lax.dynamic_index_in_dim(last, 1 - zh, 0, keepdims=False)
    last_got = swap(
        jnp.concatenate([last_sent, jnp.pad(gain_line, ((0, 60), (0, 0)))], axis=1).astype(bfloat),
        "zh",
    ).astype(single)
    gain_line = head_sum(gain_line + last_got[:4, 1024:])

    def shard(own, got, start, count):
        return in_order(zh, own[:, start : start + count], got[:, start : start + count], 1)

    shard_igate = shard(part_own, part_got, 0, 768)
    shard_ilift = shard(part_own, part_got, 768, 768)
    shard_idown = shard(part_own, part_got, 1536, 768).T
    shard_out = shard(last_own, last_got, 0, 256).T
    shard_gate = shard(last_own, last_got, 256, 256)
    shard_query = shard(last_own, last_got, 512, 256)
    shard_key = shard(last_own, last_got, 768, 128)
    shard_value = shard(last_own, last_got, 896, 128)

    gain_own = lax.dynamic_index_in_dim(gain_line[:2].reshape(2, 2, 64), zh, 1, keepdims=False)
    gain_sides = lax.dynamic_slice_in_dim(gain_line[2:], seq_index * 4, 4, 1)

    return (
        result,
        tokens_grad,
        shard_query,
        shard_key,
        shard_value,
        shard_gate,
        shard_out,
        gain_own[0],
        gain_sides[0],
        gain_sides[1],
        shard_igate,
        shard_ilift,
        shard_idown,
        gain_own[1],
    )


def solution(mesh):
    fine = Mesh(mesh.devices.reshape(2, 4, 4, 2, 2), ("zh", "y", "x", "zl", "c"))
    seq = ("zh", "y", "x")
    head = ("zl", "c")
    in_specs = (
        P(seq, None),
        P(seq, head),
        P(seq, head),
        P(seq, head),
        P(seq, head),
        P(head, seq),
        P(seq),
        P(seq),
        P(seq),
        P(seq, head),
        P(seq, head),
        P(head, seq),
        P(seq),
        P(seq, None),
        P(),
        P(),
        P(),
    )
    out_specs = (
        P(seq, None),
        P(seq, None),
        P(seq, head),
        P(seq, head),
        P(seq, head),
        P(seq, head),
        P(head, seq),
        P(seq),
        P(seq),
        P(seq),
        P(seq, head),
        P(seq, head),
        P(head, seq),
        P(seq),
    )
    return jax.shard_map(
        per_device, mesh=fine, in_specs=in_specs, out_specs=out_specs, check_vma=False
    )
```

profile of v0, /device:TPU:1, one launch (start us, length us, event | category | flops | bytes accessed | tf_op | source)
XLA Modules:
  0.0 452.6 jit_solution(15115921590752097476)
XLA Ops:
  13.6 4.4 collective-permute-start
  22.3 2.7 stack.104.info
  26.4 2.5 collective-permute-start.2
  30.0 2.7 collective-permute-start.5
  35.2 2.6 collective-permute-done.6
  38.8 2.2 collective-permute-start.11
  42.1 5.9 %collective-permute-done.11.refs_7_ = bf16[4,128,256]{2,1,0:T(8,128)(2,1)S(1)} collective-permute-done((bf16[4,128,256]{2,1,0:T(8,128)(2,1)S(1)}, bf16[4,128,256]{2,1,0:T(8,128)(2,1)S(1)}, u32[]{:S(2)}, u32[]{:S(2)}) %collective-permute-start.11) | collective-permute-done | bytes 262176 | tf_op jit(solution)/shard_map/ppermute | solution.py:61
  50.5 6.5 %collective-permute-done.13.refs_9_ = bf16[4,128,256]{2,1,0:T(8,128)(2,1)S(1)} collective-permute-done((bf16[4,128,256]{2,1,0:T(8,128)(2,1)S(1)}, bf16[4,128,256]{2,1,0:T(8,128)(2,1)S(1)}, u32[]{:S(2)}, u32[]{:S(2)}) %collective-permute-start.13) | collective-permute-done | bytes 262176 | tf_op jit(solution)/shard_map/ppermute | solution.py:61
  57.6 4.9 %project_pairs.1 = (bf16[512,2048]{1,0:T(8,128)(2,1)S(1)}, bf16[512,128]{1,0:T(8,128)(2,1)S(1)}, bf16[512,128]{1,0:T(8,128)(2,1)S(1)}, f32[512,128]{1,0:T(8,128)...) custom-call(s32[10]{0:T(128)S(1)} %stack.104.info, ...), custom_call_target="tpu_custom_call" | custom-call | flops 1073741824 | bytes 8388608 | tf_op jit(solution)/shard_map/project_pairs/pallas_call | solution.py:453
  63.7 3.0 collective-permute-start.20
  66.7 3.4 collective-permute-start.14
  71.8 3.8 collective-permute-start.17
  85.5 2.7 collective-permute-start.24
  91.5 2.9 collective-permute-done.24.refs_7_.refs_12_
  94.4 3.1 collective-permute-done.25.refs_10_.refs_15_
  97.6 3.5 collective-permute-done.23.refs_5_.refs_10_
  104.8 2.7 collective-permute-start.28
  108.2 3.0 arrange.1.refs_1_
  116.8 4.3 collective-permute-done.29.refs_9_.refs_14_
  121.1 4.9 %attend.1 = (f32[512,256]{1,0:T(8,128)S(1)}, f32[2,1,512]{2,1,0:T(1,128)S(1)}) custom-call(s32[10]{0:T(128)S(1)} %copy-done.25, s32[32]{0:T(128)S(1)} %copy-done.26, bf16[512,256]{1,0:T(8,128)(2,1)} %copy-done.28, bf16[4,512,128]{2,1,0:T(8,128)(2,1)} %copy-done.51, bf16[4,512,128]{2,1,0:T(8,128)(2,1)} %copy-done.62, ...), custom_call_target="tpu_custom_call" | custom-call | flops 4294967296 | bytes 6291456 | tf_op jit(solution)/shard_map/attend/pallas_call | solution.py:500
  129.1 25.4 %collective-permute-start.30 = (bf16[256,2048]{1,0:T(8,128)(2,1)}, bf16[256,2048]{1,0:T(8,128)(2,1)}, u32[]{:S(2)}, u32[]{:S(2)}) collective-permute-start(bf16[256,2048]{1,0:T(8,128)(2,1)} %convolution_convert_fusion), channel_id=1, source_target_pairs={{0,1},{1,0},{2,3},{3,2},{4,5},{5,4},{6,7},{7,6},{8,9},{9,8},{10,11... | collective-permute-start | bytes 3145736 | tf_op jit(solution)/shard_map/ppermute | solution.py:31
  154.6 2.6 collective-permute-done.30
  160.6 2.4 collective-permute-start.33
  163.0 3.7 collective-permute-done.31
  166.8 5.5 %collective-permute-done.32 = bf16[64,2048]{1,0:T(8,128)(2,1)S(1)} collective-permute-done((bf16[64,2048]{1,0:T(8,128)(2,1)S(1)}, bf16[64,2048]{1,0:T(8,128)(2,1)S(1)}, u32[]{:S(2)}, u32[]{:S(2)}) %collective-permute-start.32) | collective-permute-done | bytes 262176 | tf_op jit(solution)/shard_map/ppermute | solution.py:31
  177.2 3.6 collective-permute-start.35
  183.2 7.7 %collective-permute-done.35 = bf16[64,2048]{1,0:T(8,128)(2,1)S(1)} collective-permute-done((bf16[64,2048]{1,0:T(8,128)(2,1)S(1)}, bf16[64,2048]{1,0:T(8,128)(2,1)S(1)}, u32[]{:S(2)}, u32[]{:S(2)}) %collective-permute-start.35) | collective-permute-done | bytes 262176 | tf_op jit(solution)/shard_map/ppermute | solution.py:31
  190.9 3.3 collective-permute-done.36
  194.3 2.7 collective-permute-start.37
  200.3 6.3 %fusion.4 = f32[512,1536]{1,0:T(8,128)S(1)} fusion(bf16[512,2048]{1,0:T(8,128)(2,1)} %constant_dynamic-update-slice_fusion.14.refs_0_, bf16[2048,2304]{1,0:T(8,128)(2,1)} %bitcast.155), kind=kOutput, calls=%fused_computation.4 | convolution fusion | flops 3221225472 | bytes 11534336 | tf_op jit(solution)/shard_map/dot_general | solution.py:791
  207.1 2.3 multiply_convert_fusion.2
  211.7 2.3 collective-permute-done.38
  218.9 2.4 collective-permute-start.41
  221.3 12.1 %plane_grads.3 = bf16[16,128,2304]{2,1,0:T(8,128)(2,1)} custom-call(bf16[512,2048]{1,0:T(8,128)(2,1)} %constant_dynamic-update-slice_fusion.14.refs_0_, bf16[512,2048]{1,0:T(8,128)(2,1)S(1)} %copy-done.11, bf16[512,768]{1,0:T(8,128)(2,1)S(1)} %get-tuple-element.150.refs_2_, bf16[512,768]{1,0:T(8,128)(2,1)S(1)} %get-tuple-element.151.refs_3_, ...), custom_call_target="tpu_custom_call" | custom-call | flops 4831838208 | bytes 13893632 | tf_op jit(solution)/shard_map/plane_grads/pallas_call | solution.py:608
  235.3 2.4 constant_dynamic-update-slice_fusion.23
  237.7 3.1 collective-permute-start.43
  241.8 2.4 collective-permute-done.42
  244.2 6.7 %collective-permute-done.43 = bf16[64,2048]{1,0:T(8,128)(2,1)S(1)} collective-permute-done((bf16[64,2048]{1,0:T(8,128)(2,1)S(1)}, bf16[64,2048]{1,0:T(8,128)(2,1)S(1)}, u32[]{:S(2)}, u32[]{:S(2)}) %collective-permute-start.43) | collective-permute-done | bytes 262176 | tf_op jit(solution)/shard_map/ppermute | solution.py:31
  250.9 3.6 collective-permute-done.44
  260.5 9.1 %attend_back.1 = (bf16[512,256]{1,0:T(8,128)(2,1)S(1)}, f32[1,128]{1,0:T(1,128)S(1)}, bf16[4,512,128]{2,1,0:T(8,128)(2,1)}, bf16[4,512,128]{2,1,0:T(8,128)(2,1)}...) custom-call(s32[10]{0:T(128)S(1)} %copy-done.25, ...), custom_call_target="tpu_custom_call" | custom-call | flops 10737418240 | bytes 12582912 | tf_op jit(solution)/shard_map/attend_back/pallas_call | solution.py:523
  269.6 11.5 %collective-permute-start.46 = (bf16[2,512,128]{2,1,0:T(8,128)(2,1)}, bf16[2,512,128]{2,1,0:T(8,128)(2,1)S(1)}, u32[]{:S(2)}, u32[]{:S(2)}) collective-permute-start(bf16[2,512,128]{2,1,0:T(8,128)(2,1)} %get-tuple-element.159), channel_id=1, source_target_pairs={{0,4},{4,8},{8,12},{12,0},{1,5},{5,9},{9,13},{13,1},{2,6},{6,10},{... | collective-permute-start | bytes 786440 | tf_op jit(solution)/shard_map/ppermute | solution.py:61
  281.2 8.5 %collective-permute-start.48 = (bf16[2,512,128]{2,1,0:T(8,128)(2,1)}, bf16[2,512,128]{2,1,0:T(8,128)(2,1)S(1)}, u32[]{:S(2)}, u32[]{:S(2)}) collective-permute-start(bf16[2,512,128]{2,1,0:T(8,128)(2,1)} %get-tuple-element.161), channel_id=1, source_target_pairs={{0,16},{16,32},{32,48},{48,0},{1,17},{17,33},{33,49},{49,1},{2,18}... | collective-permute-start | bytes 786440 | tf_op jit(solution)/shard_map/ppermute | solution.py:61
  290.0 4.5 plane_grads.4
  294.5 6.7 %collective-permute-done.48.refs_5_ = bf16[2,512,128]{2,1,0:T(8,128)(2,1)S(1)} collective-permute-done((bf16[2,512,128]{2,1,0:T(8,128)(2,1)}, bf16[2,512,128]{2,1,0:T(8,128)(2,1)S(1)}, u32[]{:S(2)}, u32[]{:S(2)}) %collective-permute-start.48) | collective-permute-done | bytes 262176 | tf_op jit(solution)/shard_map/ppermute | solution.py:61
  301.3 6.3 %collective-permute-done.49.refs_7_ = bf16[2,512,128]{2,1,0:T(8,128)(2,1)S(1)} collective-permute-done((bf16[2,512,128]{2,1,0:T(8,128)(2,1)}, bf16[2,512,128]{2,1,0:T(8,128)(2,1)S(1)}, u32[]{:S(2)}, u32[]{:S(2)}) %collective-permute-start.49) | collective-permute-done | bytes 262176 | tf_op jit(solution)/shard_map/ppermute | solution.py:61
  307.9 2.7 collective-permute-start.51
  310.6 2.7 collective-permute-start.53
  315.4 6.0 %collective-permute-done.50 = bf16[4,512,128]{2,1,0:T(8,128)(2,1)S(1)} collective-permute-done((bf16[4,512,128]{2,1,0:T(8,128)(2,1)S(1)}, bf16[4,512,128]{2,1,0:T(8,128)(2,1)S(1)}, u32[]{:S(2)}, u32[]{:S(2)}) %collective-permute-start.50) | collective-permute-done | bytes 524320 | tf_op jit(solution)/shard_map/ppermute | solution.py:61
  329.2 4.7 %collective-permute-start.55 = (bf16[512,128]{1,0:T(8,128)(2,1)S(1)}, bf16[512,128]{1,0:T(8,128)(2,1)S(1)}, u32[]{:S(2)}, u32[]{:S(2)}) collective-permute-start(bf16[512,128]{1,0:T(8,128)(2,1)S(1)} %get-tuple-element.280), channel_id=1, source_target_pairs={{0,32},{16,48},{32,0},{48,16},{1,33},{17,49},{33,1},{49,17},{2,34}... | collective-permute-start | bytes 393224 | tf_op jit(solution)/shard_map/ppermute | solution.py:61
  336.3 3.0 collective-permute-start.56
  346.6 6.8 %collective-permute-start.60 = (bf16[256,2048]{1,0:T(8,128)(2,1)S(1)}, bf16[256,2048]{1,0:T(8,128)(2,1)S(1)}, u32[]{:S(2)}, u32[]{:S(2)}) collective-permute-start(bf16[256,2048]{1,0:T(8,128)(2,1)S(1)} %add_convert_fusion), channel_id=1, source_target_pairs={{0,1},{1,0},{2,3},{3,2},{4,5},{5,4},{6,7},{7,6},{8,9},{9,8},{10,11... | collective-permute-start | bytes 3145736 | tf_op jit(solution)/shard_map/ppermute | solution.py:31
  357.4 3.9 convolution_convert_fusion.1
  362.6 5.2 %all-to-all-start = ((bf16[16,144,256]{2,1,0:T(8,128)(2,1)}), bf16[16,144,256]{2,1,0:T(8,128)(2,1)}, u32[]{:S(2)}, u32[]{:S(2)}) async-start(bf16[16,144,256]{2,1,0:T(8,128)(2,1)} %plane_grads.5), calls=%async_computation | async-start | bytes 2359296 | tf_op jit(solution)/shard_map/all_to_all | solution.py:875
  368.9 3.0 collective-permute-start.68
  371.9 4.6 %fusion.115 = (bf16[256,2048]{1,0:T(8,128)(2,1)S(1)}, f32[256,2048]{1,0:T(8,128)}) fusion(bf16[256,2048]{1,0:T(8,128)(2,1)} %collective-permute-done.61, bf16[2048,2304]{1,0:T(8,128)(2,1)} %bitcast.157, bf16[512,768]{1,0:T(8,128)(2,1)S(1)} %copy-done.23), kind=kOutput, calls=%fused_computation.281 | convolution fusion | flops 806879232 | bytes 7733248 | tf_op jit(solution)/shard_map/dot_general | solution.py:241
  378.5 2.7 collective-permute-start.64
  381.2 2.2 collective-permute-done.68
  384.9 9.5 %reduce-scatter.6.cloned.1.call-done = bf16[1,4,128,768]{3,2,1,0:T(8,128)(2,1)} async-done(((bf16[4,4,128,768]{3,2,1,0:T(8,128)(2,1)}), bf16[1,4,128,768]{3,2,1,0:T(8,128)(2,1)}) %reduce-scatter.6.cloned.1.call-update) | async-done | bytes 786448 | tf_op jit(solution)/shard_map/reduce_scatter | solution.py:859
  396.2 2.7 collective-permute-start.65
  400.0 2.6 collective-permute-start.69
  405.8 7.6 %collective-permute-done.69 = bf16[64,2304]{1,0:T(8,128)(2,1)S(1)} collective-permute-done((bf16[64,2304]{1,0:T(8,128)(2,1)S(1)}, bf16[64,2304]{1,0:T(8,128)(2,1)S(1)}, u32[]{:S(2)}, u32[]{:S(2)}) %collective-permute-start.69) | collective-permute-done | bytes 294944 | tf_op jit(solution)/shard_map/ppermute | solution.py:31
  413.5 6.0 %reduce-scatter.8.cloned.1.call-done = bf16[1,128,768]{2,1,0:T(8,128)(2,1)} async-done(((bf16[4,128,768]{2,1,0:T(8,128)(2,1)}), bf16[1,128,768]{2,1,0:T(8,128)(2,1)}) %reduce-scatter.8.cloned.1.call-update) | async-done | bytes 196624 | tf_op jit(solution)/shard_map/reduce_scatter | solution.py:862
  424.4 2.9 collective-permute-start.73
  428.9 2.3 collective-permute-start.70
  (406 shorter events, 136.9 us)
Async XLA Ops:
  7.2 104.1 %all-gather.3.cloned.1.call-start = ((), (), s32[]{:S(2)}) async-start(), calls=%async_computation.4 | async-start | bytes 3342336 | tf_op jit(solution)/shard_map/all_gather | solution.py:649
  13.6 11.6 %collective-permute-start = (bf16[64,1280]{1,0:T(8,128)(2,1)S(1)}, bf16[64,1280]{1,0:T(8,128)(2,1)S(1)}, u32[]{:S(2)}, u32[]{:S(2)}) collective-permute-start(bf16[64,1280]{1,0:T(8,128)(2,1)S(1)} %get-tuple-element.299), channel_id=1, source_target_pairs={{0,64},{64,0},{1,65},{65,1},{2,66},{66,2},{3,67},{67,3},{4,68},{68... | collective-permute-start | bytes 491528 | tf_op jit(solution)/shard_map/ppermute | solution.py:31
  26.1 174.1 %all-gather.5.cloned.1.call-start = ((), (), s32[]{:S(2)}) async-start(), calls=%async_computation.5 | async-start | bytes 10027008 | tf_op jit(solution)/shard_map/all_gather | solution.py:649
  26.2 31.4 %collective-permute-start.1 = (bf16[256,2048]{1,0:T(8,128)(2,1)S(1)}, bf16[256,2048]{1,0:T(8,128)(2,1)}, u32[]{:S(2)}, u32[]{:S(2)}) collective-permute-start(bf16[256,2048]{1,0:T(8,128)(2,1)S(1)} %copy-done.36), channel_id=1, source_target_pairs={{0,64},{64,0},{1,65},{65,1},{2,66},{66,2},{3,67},{67,3},{4,68},{68... | collective-permute-start | bytes 3145736 | tf_op jit(solution)/shard_map/ppermute | solution.py:31
  38.8 9.2 %collective-permute-start.11 = (bf16[4,128,256]{2,1,0:T(8,128)(2,1)S(1)}, bf16[4,128,256]{2,1,0:T(8,128)(2,1)S(1)}, u32[]{:S(2)}, u32[]{:S(2)}) collective-permute-start(bf16[4,128,256]{2,1,0:T(8,128)(2,1)S(1)} %pad_maximum_fusion.22.refs_6_), channel_id=1, source_target_pairs={{0,12},{4,0},{8,4},{12,8},{1,13},{5,1},{9,5},{13,9},{2,14},{6,2},{... | collective-permute-start | bytes 786440 | tf_op jit(solution)/shard_map/ppermute | solution.py:61
  41.0 8.2 %collective-permute-start.12 = (bf16[4,128,256]{2,1,0:T(8,128)(2,1)S(1)}, bf16[4,128,256]{2,1,0:T(8,128)(2,1)S(1)}, u32[]{:S(2)}, u32[]{:S(2)}) collective-permute-start(bf16[4,128,256]{2,1,0:T(8,128)(2,1)S(1)} %pad_maximum_fusion.22.refs_6_), channel_id=1, source_target_pairs={{0,8},{4,12},{8,0},{12,4},{1,9},{5,13},{9,1},{13,5},{2,10},{6,14},... | collective-permute-start | bytes 786440 | tf_op jit(solution)/shard_map/ppermute | solution.py:61
  41.9 15.0 %collective-permute-start.13 = (bf16[4,128,256]{2,1,0:T(8,128)(2,1)S(1)}, bf16[4,128,256]{2,1,0:T(8,128)(2,1)S(1)}, u32[]{:S(2)}, u32[]{:S(2)}) collective-permute-start(bf16[4,128,256]{2,1,0:T(8,128)(2,1)S(1)} %pad_maximum_fusion.22.refs_6_), channel_id=1, source_target_pairs={{0,4},{4,8},{8,12},{12,0},{1,5},{5,9},{9,13},{13,1},{2,6},{6,10},{... | collective-permute-start | bytes 786440 | tf_op jit(solution)/shard_map/ppermute | solution.py:61
  42.0 15.0 %collective-permute-start.10 = (bf16[4,128,256]{2,1,0:T(8,128)(2,1)S(1)}, bf16[4,128,256]{2,1,0:T(8,128)(2,1)}, u32[]{:S(2)}, u32[]{:S(2)}) collective-permute-start(bf16[4,128,256]{2,1,0:T(8,128)(2,1)S(1)} %pad_maximum_fusion.21.refs_2_), channel_id=1, source_target_pairs={{0,16},{16,32},{32,48},{48,0},{1,17},{17,33},{33,49},{49,1},{2,18}... | collective-permute-start | bytes 786440 | tf_op jit(solution)/shard_map/ppermute | solution.py:61
  48.0 8.9 %collective-permute-start.8 = (bf16[4,128,256]{2,1,0:T(8,128)(2,1)S(1)}, bf16[4,128,256]{2,1,0:T(8,128)(2,1)}, u32[]{:S(2)}, u32[]{:S(2)}) collective-permute-start(bf16[4,128,256]{2,1,0:T(8,128)(2,1)S(1)} %pad_maximum_fusion.21.refs_2_), channel_id=1, source_target_pairs={{0,48},{16,0},{32,16},{48,32},{1,49},{17,1},{33,17},{49,33},{2,50}... | collective-permute-start | bytes 786440 | tf_op jit(solution)/shard_map/ppermute | solution.py:61
  49.2 7.8 %collective-permute-start.9 = (bf16[4,128,256]{2,1,0:T(8,128)(2,1)S(1)}, bf16[4,128,256]{2,1,0:T(8,128)(2,1)}, u32[]{:S(2)}, u32[]{:S(2)}) collective-permute-start(bf16[4,128,256]{2,1,0:T(8,128)(2,1)S(1)} %pad_maximum_fusion.21.refs_2_), channel_id=1, source_target_pairs={{0,32},{16,48},{32,0},{48,16},{1,33},{17,49},{33,1},{49,17},{2,34}... | collective-permute-start | bytes 786440 | tf_op jit(solution)/shard_map/ppermute | solution.py:61
  63.7 11.9 %collective-permute-start.20 = (bf16[64,2304]{1,0:T(8,128)(2,1)S(1)}, bf16[64,2304]{1,0:T(8,128)(2,1)S(1)}, u32[]{:S(2)}, u32[]{:S(2)}) collective-permute-start(bf16[64,2304]{1,0:T(8,128)(2,1)S(1)} %pad_maximum_fusion.16), channel_id=1, source_target_pairs={{0,64},{64,0},{1,65},{65,1},{2,66},{66,2},{3,67},{67,3},{4,68},{68... | collective-permute-start | bytes 884744 | tf_op jit(solution)/shard_map/ppermute | solution.py:31
  66.7 9.7 %collective-permute-start.14 = (bf16[512,128]{1,0:T(8,128)(2,1)S(1)}, bf16[512,128]{1,0:T(8,128)(2,1)S(1)}, u32[]{:S(2)}, u32[]{:S(2)}) collective-permute-start(bf16[512,128]{1,0:T(8,128)(2,1)S(1)} %get-tuple-element.126), channel_id=1, source_target_pairs={{0,12},{4,0},{8,4},{12,8},{1,13},{5,1},{9,5},{13,9},{2,14},{6,2},{... | collective-permute-start | bytes 393224 | tf_op jit(solution)/shard_map/ppermute | solution.py:61
  70.1 9.5 %collective-permute-start.15 = (bf16[512,128]{1,0:T(8,128)(2,1)S(1)}, bf16[512,128]{1,0:T(8,128)(2,1)}, u32[]{:S(2)}, u32[]{:S(2)}) collective-permute-start(bf16[512,128]{1,0:T(8,128)(2,1)S(1)} %get-tuple-element.126), channel_id=1, source_target_pairs={{0,8},{4,12},{8,0},{12,4},{1,9},{5,13},{9,1},{13,5},{2,10},{6,14},... | collective-permute-start | bytes 393224 | tf_op jit(solution)/shard_map/ppermute | solution.py:61
  71.8 8.8 %collective-permute-start.16 = (bf16[512,128]{1,0:T(8,128)(2,1)S(1)}, bf16[512,128]{1,0:T(8,128)(2,1)}, u32[]{:S(2)}, u32[]{:S(2)}) collective-permute-start(bf16[512,128]{1,0:T(8,128)(2,1)S(1)} %get-tuple-element.126), channel_id=1, source_target_pairs={{0,4},{4,8},{8,12},{12,0},{1,5},{5,9},{9,13},{13,1},{2,6},{6,10},{... | collective-permute-start | bytes 393224 | tf_op jit(solution)/shard_map/ppermute | solution.py:61
  71.8 8.8 %collective-permute-start.17 = (bf16[512,128]{1,0:T(8,128)(2,1)S(1)}, bf16[512,128]{1,0:T(8,128)(2,1)}, u32[]{:S(2)}, u32[]{:S(2)}) collective-permute-start(bf16[512,128]{1,0:T(8,128)(2,1)S(1)} %get-tuple-element.127), channel_id=1, source_target_pairs={{0,48},{16,0},{32,16},{48,32},{1,49},{17,1},{33,17},{49,33},{2,50}... | collective-permute-start | bytes 393224 | tf_op jit(solution)/shard_map/ppermute | solution.py:61
  82.7 259.5 %reduce-scatter.10.cloned.1.call-start = ((), (), s32[]{:S(2)}) async-start(), calls=%async_computation.8 | async-start | bytes 10027008
  82.8 25.4 %collective-permute-start.21 = (bf16[256,2048]{1,0:T(8,128)(2,1)}, bf16[256,2048]{1,0:T(8,128)(2,1)}, u32[]{:S(2)}, u32[]{:S(2)}) collective-permute-start(bf16[256,2048]{1,0:T(8,128)(2,1)} %own.1), channel_id=1, source_target_pairs={{0,64},{64,0},{1,65},{65,1},{2,66},{66,2},{3,67},{67,3},{4,68},{68... | collective-permute-start | bytes 3145736 | tf_op jit(solution)/shard_map/ppermute | solution.py:31
  85.5 8.8 %collective-permute-start.24 = (bf16[4,512,128]{2,1,0:T(8,128)(2,1)S(1)}, bf16[4,512,128]{2,1,0:T(8,128)(2,1)S(1)}, u32[]{:S(2)}, u32[]{:S(2)}) collective-permute-start(bf16[4,512,128]{2,1,0:T(8,128)(2,1)S(1)} %pad_maximum_fusion.8.refs_6_.refs_11_), channel_id=1, source_target_pairs={{0,12},{4,0},{8,4},{12,8},{1,13},{5,1},{9,5},{13,9},{2,14},{6,2},{... | collective-permute-start | bytes 1572872 | tf_op jit(solution)/shard_map/ppermute | solution.py:61
  88.2 9.2 %collective-permute-start.25 = (bf16[4,512,128]{2,1,0:T(8,128)(2,1)S(1)}, bf16[4,512,128]{2,1,0:T(8,128)(2,1)S(1)}, u32[]{:S(2)}, u32[]{:S(2)}) collective-permute-start(bf16[4,512,128]{2,1,0:T(8,128)(2,1)S(1)} %pad_maximum_fusion.8.refs_6_.refs_11_), channel_id=1, source_target_pairs={{0,4},{4,8},{8,12},{12,0},{1,5},{5,9},{9,13},{13,1},{2,6},{6,10},{... | collective-permute-start | bytes 1572872 | tf_op jit(solution)/shard_map/ppermute | solution.py:61
  89.3 8.3 %collective-permute-start.22 = (bf16[4,512,128]{2,1,0:T(8,128)(2,1)S(1)}, bf16[4,512,128]{2,1,0:T(8,128)(2,1)S(1)}, u32[]{:S(2)}, u32[]{:S(2)}) collective-permute-start(bf16[4,512,128]{2,1,0:T(8,128)(2,1)S(1)} %pad_maximum_fusion.7.refs_1_.refs_6_), channel_id=1, source_target_pairs={{0,48},{16,0},{32,16},{48,32},{1,49},{17,1},{33,17},{49,33},{2,50}... | collective-permute-start | bytes 1572872 | tf_op jit(solution)/shard_map/ppermute | solution.py:61
  91.5 9.6 %collective-permute-start.23 = (bf16[4,512,128]{2,1,0:T(8,128)(2,1)S(1)}, bf16[4,512,128]{2,1,0:T(8,128)(2,1)S(1)}, u32[]{:S(2)}, u32[]{:S(2)}) collective-permute-start(bf16[4,512,128]{2,1,0:T(8,128)(2,1)S(1)} %pad_maximum_fusion.7.refs_1_.refs_6_), channel_id=1, source_target_pairs={{0,16},{16,32},{32,48},{48,0},{1,17},{17,33},{33,49},{49,1},{2,18}... | collective-permute-start | bytes 1572872 | tf_op jit(solution)/shard_map/ppermute | solution.py:61
  101.9 14.9 %collective-permute-start.26 = (bf16[2,512,128]{2,1,0:T(8,128)(2,1)}, bf16[2,512,128]{2,1,0:T(8,128)(2,1)}, u32[]{:S(2)}, u32[]{:S(2)}) collective-permute-start(bf16[2,512,128]{2,1,0:T(8,128)(2,1)} %slice.302), channel_id=1, source_target_pairs={{0,48},{16,0},{32,16},{48,32},{1,49},{17,1},{33,17},{49,33},{2,50}... | collective-permute-start | bytes 786440 | tf_op jit(solution)/shard_map/ppermute | solution.py:61
  102.6 14.1 %collective-permute-start.27 = (bf16[2,512,128]{2,1,0:T(8,128)(2,1)}, bf16[2,512,128]{2,1,0:T(8,128)(2,1)}, u32[]{:S(2)}, u32[]{:S(2)}) collective-permute-start(bf16[2,512,128]{2,1,0:T(8,128)(2,1)} %slice.303), channel_id=1, source_target_pairs={{0,16},{16,32},{32,48},{48,0},{1,17},{17,33},{33,49},{49,1},{2,18}... | collective-permute-start | bytes 786440 | tf_op jit(solution)/shard_map/ppermute | solution.py:61
  104.8 12.0 %collective-permute-start.28 = (bf16[2,512,128]{2,1,0:T(8,128)(2,1)}, bf16[2,512,128]{2,1,0:T(8,128)(2,1)}, u32[]{:S(2)}, u32[]{:S(2)}) collective-permute-start(bf16[2,512,128]{2,1,0:T(8,128)(2,1)} %slice.304), channel_id=1, source_target_pairs={{0,12},{4,0},{8,4},{12,8},{1,13},{5,1},{9,5},{13,9},{2,14},{6,2},{... | collective-permute-start | bytes 786440 | tf_op jit(solution)/shard_map/ppermute | solution.py:61
  108.2 12.9 %collective-permute-start.29 = (bf16[2,512,128]{2,1,0:T(8,128)(2,1)}, bf16[2,512,128]{2,1,0:T(8,128)(2,1)}, u32[]{:S(2)}, u32[]{:S(2)}) collective-permute-start(bf16[2,512,128]{2,1,0:T(8,128)(2,1)} %slice.305), channel_id=1, source_target_pairs={{0,4},{4,8},{8,12},{12,0},{1,5},{5,9},{9,13},{13,1},{2,6},{6,10},{... | collective-permute-start | bytes 786440 | tf_op jit(solution)/shard_map/ppermute | solution.py:61
  129.1 28.1 %collective-permute-start.30 = (bf16[256,2048]{1,0:T(8,128)(2,1)}, bf16[256,2048]{1,0:T(8,128)(2,1)}, u32[]{:S(2)}, u32[]{:S(2)}) collective-permute-start(bf16[256,2048]{1,0:T(8,128)(2,1)} %convolution_convert_fusion), channel_id=1, source_target_pairs={{0,1},{1,0},{2,3},{3,2},{4,5},{5,4},{6,7},{7,6},{8,9},{9,8},{10,11... | collective-permute-start | bytes 3145736 | tf_op jit(solution)/shard_map/ppermute | solution.py:31
  159.7 12.6 %collective-permute-start.32 = (bf16[64,2048]{1,0:T(8,128)(2,1)S(1)}, bf16[64,2048]{1,0:T(8,128)(2,1)S(1)}, u32[]{:S(2)}, u32[]{:S(2)}) collective-permute-start(bf16[64,2048]{1,0:T(8,128)(2,1)S(1)} %get-tuple-element.261), channel_id=1, source_target_pairs={{0,64},{64,0},{1,65},{65,1},{2,66},{66,2},{3,67},{67,3},{4,68},{68... | collective-permute-start | bytes 786440 | tf_op jit(solution)/shard_map/ppermute | solution.py:31
  160.6 13.7 %collective-permute-start.33 = (bf16[64,2048]{1,0:T(8,128)(2,1)S(1)}, bf16[64,2048]{1,0:T(8,128)(2,1)S(1)}, u32[]{:S(2)}, u32[]{:S(2)}) collective-permute-start(bf16[64,2048]{1,0:T(8,128)(2,1)S(1)} %get-tuple-element.260), channel_id=1, source_target_pairs={{0,66},{2,64},{64,2},{66,0},{1,67},{3,65},{65,3},{67,1},{4,70},{6,... | collective-permute-start | bytes 786440 | tf_op jit(solution)/shard_map/ppermute | solution.py:35
  177.2 13.7 %collective-permute-start.35 = (bf16[64,2048]{1,0:T(8,128)(2,1)S(1)}, bf16[64,2048]{1,0:T(8,128)(2,1)S(1)}, u32[]{:S(2)}, u32[]{:S(2)}) collective-permute-start(bf16[64,2048]{1,0:T(8,128)(2,1)S(1)} %get-tuple-element.227), channel_id=1, source_target_pairs={{0,64},{64,0},{1,65},{65,1},{2,66},{66,2},{3,67},{67,3},{4,68},{68... | collective-permute-start | bytes 786440 | tf_op jit(solution)/shard_map/ppermute | solution.py:31
  180.8 13.4 %collective-permute-start.36 = (bf16[64,2048]{1,0:T(8,128)(2,1)S(1)}, bf16[64,2048]{1,0:T(8,128)(2,1)S(1)}, u32[]{:S(2)}, u32[]{:S(2)}) collective-permute-start(bf16[64,2048]{1,0:T(8,128)(2,1)S(1)} %get-tuple-element.227), channel_id=1, source_target_pairs={{0,66},{2,64},{64,2},{66,0},{1,67},{3,65},{65,3},{67,1},{4,70},{6,... | collective-permute-start | bytes 786440 | tf_op jit(solution)/shard_map/ppermute | solution.py:35
  217.4 16.0 %collective-permute-start.39 = (bf16[64,2048]{1,0:T(8,128)(2,1)}, bf16[64,2048]{1,0:T(8,128)(2,1)}, u32[]{:S(2)}, u32[]{:S(2)}) collective-permute-start(bf16[64,2048]{1,0:T(8,128)(2,1)} %get-tuple-element.258), channel_id=1, source_target_pairs={{0,2},{2,0},{1,3},{3,1},{4,6},{6,4},{5,7},{7,5},{8,10},{10,8},{9,1... | collective-permute-start | bytes 786440 | tf_op jit(solution)/shard_map/ppermute | solution.py:31
  217.4 16.0 %collective-permute-start.40 = (bf16[64,2048]{1,0:T(8,128)(2,1)}, bf16[64,2048]{1,0:T(8,128)(2,1)}, u32[]{:S(2)}, u32[]{:S(2)}) collective-permute-start(bf16[64,2048]{1,0:T(8,128)(2,1)} %get-tuple-element.257), channel_id=1, source_target_pairs={{0,64},{64,0},{1,65},{65,1},{2,66},{66,2},{3,67},{67,3},{4,68},{68... | collective-permute-start | bytes 786440 | tf_op jit(solution)/shard_map/ppermute | solution.py:31
  218.9 14.5 %collective-permute-start.41 = (bf16[64,2048]{1,0:T(8,128)(2,1)}, bf16[64,2048]{1,0:T(8,128)(2,1)}, u32[]{:S(2)}, u32[]{:S(2)}) collective-permute-start(bf16[64,2048]{1,0:T(8,128)(2,1)} %get-tuple-element.256), channel_id=1, source_target_pairs={{0,66},{2,64},{64,2},{66,0},{1,67},{3,65},{65,3},{67,1},{4,70},{6,... | collective-permute-start | bytes 786440 | tf_op jit(solution)/shard_map/ppermute | solution.py:35
  233.4 160.9 %reduce-scatter.6.cloned.1.call-start = ((), (), s32[]{:S(2)}) async-start(), calls=%async_computation.6 | async-start | bytes 3932160 | tf_op jit(solution)/shard_map/reduce_scatter | solution.py:859
  237.7 13.2 %collective-permute-start.43 = (bf16[64,2048]{1,0:T(8,128)(2,1)S(1)}, bf16[64,2048]{1,0:T(8,128)(2,1)S(1)}, u32[]{:S(2)}, u32[]{:S(2)}) collective-permute-start(bf16[64,2048]{1,0:T(8,128)(2,1)S(1)} %get-tuple-element.224), channel_id=1, source_target_pairs={{0,64},{64,0},{1,65},{65,1},{2,66},{66,2},{3,67},{67,3},{4,68},{68... | collective-permute-start | bytes 786440 | tf_op jit(solution)/shard_map/ppermute | solution.py:31
  240.8 13.7 %collective-permute-start.44 = (bf16[64,2048]{1,0:T(8,128)(2,1)S(1)}, bf16[64,2048]{1,0:T(8,128)(2,1)S(1)}, u32[]{:S(2)}, u32[]{:S(2)}) collective-permute-start(bf16[64,2048]{1,0:T(8,128)(2,1)S(1)} %get-tuple-element.224), channel_id=1, source_target_pairs={{0,66},{2,64},{64,2},{66,0},{1,67},{3,65},{65,3},{67,1},{4,70},{6,... | collective-permute-start | bytes 786440 | tf_op jit(solution)/shard_map/ppermute | solution.py:35
  269.6 24.9 %collective-permute-start.46 = (bf16[2,512,128]{2,1,0:T(8,128)(2,1)}, bf16[2,512,128]{2,1,0:T(8,128)(2,1)S(1)}, u32[]{:S(2)}, u32[]{:S(2)}) collective-permute-start(bf16[2,512,128]{2,1,0:T(8,128)(2,1)} %get-tuple-element.159), channel_id=1, source_target_pairs={{0,4},{4,8},{8,12},{12,0},{1,5},{5,9},{9,13},{13,1},{2,6},{6,10},{... | collective-permute-start | bytes 786440 | tf_op jit(solution)/shard_map/ppermute | solution.py:61
  281.1 13.4 %collective-permute-start.47 = (bf16[2,512,128]{2,1,0:T(8,128)(2,1)}, bf16[2,512,128]{2,1,0:T(8,128)(2,1)S(1)}, u32[]{:S(2)}, u32[]{:S(2)}) collective-permute-start(bf16[2,512,128]{2,1,0:T(8,128)(2,1)} %get-tuple-element.160), channel_id=1, source_target_pairs={{0,12},{4,0},{8,4},{12,8},{1,13},{5,1},{9,5},{13,9},{2,14},{6,2},{... | collective-permute-start | bytes 786440 | tf_op jit(solution)/shard_map/ppermute | solution.py:61
  281.2 20.1 %collective-permute-start.48 = (bf16[2,512,128]{2,1,0:T(8,128)(2,1)}, bf16[2,512,128]{2,1,0:T(8,128)(2,1)S(1)}, u32[]{:S(2)}, u32[]{:S(2)}) collective-permute-start(bf16[2,512,128]{2,1,0:T(8,128)(2,1)} %get-tuple-element.161), channel_id=1, source_target_pairs={{0,16},{16,32},{32,48},{48,0},{1,17},{17,33},{33,49},{49,1},{2,18}... | collective-permute-start | bytes 786440 | tf_op jit(solution)/shard_map/ppermute | solution.py:61
  289.6 17.9 %collective-permute-start.49 = (bf16[2,512,128]{2,1,0:T(8,128)(2,1)}, bf16[2,512,128]{2,1,0:T(8,128)(2,1)S(1)}, u32[]{:S(2)}, u32[]{:S(2)}) collective-permute-start(bf16[2,512,128]{2,1,0:T(8,128)(2,1)} %get-tuple-element.162), channel_id=1, source_target_pairs={{0,48},{16,0},{32,16},{48,32},{1,49},{17,1},{33,17},{49,33},{2,50}... | collective-permute-start | bytes 786440 | tf_op jit(solution)/shard_map/ppermute | solution.py:61
  307.9 13.5 %collective-permute-start.50 = (bf16[4,512,128]{2,1,0:T(8,128)(2,1)S(1)}, bf16[4,512,128]{2,1,0:T(8,128)(2,1)S(1)}, u32[]{:S(2)}, u32[]{:S(2)}) collective-permute-start(bf16[4,512,128]{2,1,0:T(8,128)(2,1)S(1)} %get-tuple-element.171), channel_id=1, source_target_pairs={{0,4},{4,8},{8,12},{12,0},{1,5},{5,9},{9,13},{13,1},{2,6},{6,10},{... | collective-permute-start | bytes 1572872 | tf_op jit(solution)/shard_map/ppermute | solution.py:61
  307.9 13.4 %collective-permute-start.51 = (bf16[4,512,128]{2,1,0:T(8,128)(2,1)S(1)}, bf16[4,512,128]{2,1,0:T(8,128)(2,1)S(1)}, u32[]{:S(2)}, u32[]{:S(2)}) collective-permute-start(bf16[4,512,128]{2,1,0:T(8,128)(2,1)S(1)} %get-tuple-element.172), channel_id=1, source_target_pairs={{0,12},{4,0},{8,4},{12,8},{1,13},{5,1},{9,5},{13,9},{2,14},{6,2},{... | collective-permute-start | bytes 1572872 | tf_op jit(solution)/shard_map/ppermute | solution.py:61
  310.6 12.8 %collective-permute-start.52 = (bf16[4,512,128]{2,1,0:T(8,128)(2,1)S(1)}, bf16[4,512,128]{2,1,0:T(8,128)(2,1)S(1)}, u32[]{:S(2)}, u32[]{:S(2)}) collective-permute-start(bf16[4,512,128]{2,1,0:T(8,128)(2,1)S(1)} %get-tuple-element.173), channel_id=1, source_target_pairs={{0,16},{16,32},{32,48},{48,0},{1,17},{17,33},{33,49},{49,1},{2,18}... | collective-permute-start | bytes 1572872 | tf_op jit(solution)/shard_map/ppermute | solution.py:61
  310.6 14.2 %collective-permute-start.53 = (bf16[4,512,128]{2,1,0:T(8,128)(2,1)S(1)}, bf16[4,512,128]{2,1,0:T(8,128)(2,1)S(1)}, u32[]{:S(2)}, u32[]{:S(2)}) collective-permute-start(bf16[4,512,128]{2,1,0:T(8,128)(2,1)S(1)} %get-tuple-element.174), channel_id=1, source_target_pairs={{0,48},{16,0},{32,16},{48,32},{1,49},{17,1},{33,17},{49,33},{2,50}... | collective-permute-start | bytes 1572872 | tf_op jit(solution)/shard_map/ppermute | solution.py:61
  326.1 9.5 %collective-permute-start.57 = (bf16[512,128]{1,0:T(8,128)(2,1)S(1)}, bf16[512,128]{1,0:T(8,128)(2,1)S(1)}, u32[]{:S(2)}, u32[]{:S(2)}) collective-permute-start(bf16[512,128]{1,0:T(8,128)(2,1)S(1)} %get-tuple-element.278), channel_id=1, source_target_pairs={{0,4},{4,8},{8,12},{12,0},{1,5},{5,9},{9,13},{13,1},{2,6},{6,10},{... | collective-permute-start | bytes 393224 | tf_op jit(solution)/shard_map/ppermute | solution.py:61
  326.2 15.2 %collective-permute-start.58 = (bf16[512,128]{1,0:T(8,128)(2,1)S(1)}, bf16[512,128]{1,0:T(8,128)(2,1)S(1)}, u32[]{:S(2)}, u32[]{:S(2)}) collective-permute-start(bf16[512,128]{1,0:T(8,128)(2,1)S(1)} %get-tuple-element.277), channel_id=1, source_target_pairs={{0,8},{4,12},{8,0},{12,4},{1,9},{5,13},{9,1},{13,5},{2,10},{6,14},... | collective-permute-start | bytes 393224 | tf_op jit(solution)/shard_map/ppermute | solution.py:61
  326.6 14.8 %collective-permute-start.59 = (bf16[512,128]{1,0:T(8,128)(2,1)S(1)}, bf16[512,128]{1,0:T(8,128)(2,1)S(1)}, u32[]{:S(2)}, u32[]{:S(2)}) collective-permute-start(bf16[512,128]{1,0:T(8,128)(2,1)S(1)} %get-tuple-element.276), channel_id=1, source_target_pairs={{0,12},{4,0},{8,4},{12,8},{1,13},{5,1},{9,5},{13,9},{2,14},{6,2},{... | collective-permute-start | bytes 393224 | tf_op jit(solution)/shard_map/ppermute | solution.py:61
  329.1 12.3 %collective-permute-start.54 = (bf16[512,128]{1,0:T(8,128)(2,1)S(1)}, bf16[512,128]{1,0:T(8,128)(2,1)S(1)}, u32[]{:S(2)}, u32[]{:S(2)}) collective-permute-start(bf16[512,128]{1,0:T(8,128)(2,1)S(1)} %get-tuple-element.281), channel_id=1, source_target_pairs={{0,16},{16,32},{32,48},{48,0},{1,17},{17,33},{33,49},{49,1},{2,18}... | collective-permute-start | bytes 393224 | tf_op jit(solution)/shard_map/ppermute | solution.py:61
  329.2 12.2 %collective-permute-start.55 = (bf16[512,128]{1,0:T(8,128)(2,1)S(1)}, bf16[512,128]{1,0:T(8,128)(2,1)S(1)}, u32[]{:S(2)}, u32[]{:S(2)}) collective-permute-start(bf16[512,128]{1,0:T(8,128)(2,1)S(1)} %get-tuple-element.280), channel_id=1, source_target_pairs={{0,32},{16,48},{32,0},{48,16},{1,33},{17,49},{33,1},{49,17},{2,34}... | collective-permute-start | bytes 393224 | tf_op jit(solution)/shard_map/ppermute | solution.py:61
  346.6 9.2 %collective-permute-start.60 = (bf16[256,2048]{1,0:T(8,128)(2,1)S(1)}, bf16[256,2048]{1,0:T(8,128)(2,1)S(1)}, u32[]{:S(2)}, u32[]{:S(2)}) collective-permute-start(bf16[256,2048]{1,0:T(8,128)(2,1)S(1)} %add_convert_fusion), channel_id=1, source_target_pairs={{0,1},{1,0},{2,3},{3,2},{4,5},{5,4},{6,7},{7,6},{8,9},{9,8},{10,11... | collective-permute-start | bytes 3145736 | tf_op jit(solution)/shard_map/ppermute | solution.py:31
  361.3 10.6 %collective-permute-start.61 = (bf16[256,2048]{1,0:T(8,128)(2,1)}, bf16[256,2048]{1,0:T(8,128)(2,1)}, u32[]{:S(2)}, u32[]{:S(2)}) collective-permute-start(bf16[256,2048]{1,0:T(8,128)(2,1)} %convolution_convert_fusion.1), channel_id=1, source_target_pairs={{0,1},{1,0},{2,3},{3,2},{4,5},{5,4},{6,7},{7,6},{8,9},{9,8},{10,11... | collective-permute-start | bytes 3145736 | tf_op jit(solution)/shard_map/ppermute | solution.py:31
  362.6 50.9 %all-to-all-start = ((bf16[16,144,256]{2,1,0:T(8,128)(2,1)}), bf16[16,144,256]{2,1,0:T(8,128)(2,1)}, u32[]{:S(2)}, u32[]{:S(2)}) async-start(bf16[16,144,256]{2,1,0:T(8,128)(2,1)} %plane_grads.5), calls=%async_computation | async-start | bytes 2359296 | tf_op jit(solution)/shard_map/all_to_all | solution.py:875
  367.7 51.7 %reduce-scatter.8.cloned.1.call-start = ((), (), s32[]{:S(2)}) async-start(), calls=%async_computation.7 | async-start | bytes 983040 | tf_op jit(solution)/shard_map/reduce_scatter | solution.py:862
  368.0 10.5 %collective-permute-start.66 = (bf16[64,2048]{1,0:T(8,128)(2,1)S(1)}, bf16[64,2048]{1,0:T(8,128)(2,1)S(1)}, u32[]{:S(2)}, u32[]{:S(2)}) collective-permute-start(bf16[64,2048]{1,0:T(8,128)(2,1)S(1)} %get-tuple-element.247), channel_id=1, source_target_pairs={{0,2},{2,0},{1,3},{3,1},{4,6},{6,4},{5,7},{7,5},{8,10},{10,8},{9,1... | collective-permute-start | bytes 786440 | tf_op jit(solution)/shard_map/ppermute | solution.py:31
  368.1 13.2 %collective-permute-start.67 = (bf16[64,2048]{1,0:T(8,128)(2,1)S(1)}, bf16[64,2048]{1,0:T(8,128)(2,1)S(1)}, u32[]{:S(2)}, u32[]{:S(2)}) collective-permute-start(bf16[64,2048]{1,0:T(8,128)(2,1)S(1)} %get-tuple-element.249), channel_id=1, source_target_pairs={{0,64},{64,0},{1,65},{65,1},{2,66},{66,2},{3,67},{67,3},{4,68},{68... | collective-permute-start | bytes 786440 | tf_op jit(solution)/shard_map/ppermute | solution.py:31
  368.9 14.6 %collective-permute-start.68 = (bf16[64,2048]{1,0:T(8,128)(2,1)S(1)}, bf16[64,2048]{1,0:T(8,128)(2,1)S(1)}, u32[]{:S(2)}, u32[]{:S(2)}) collective-permute-start(bf16[64,2048]{1,0:T(8,128)(2,1)S(1)} %get-tuple-element.248), channel_id=1, source_target_pairs={{0,66},{2,64},{64,2},{66,0},{1,67},{3,65},{65,3},{67,1},{4,70},{6,... | collective-permute-start | bytes 786440 | tf_op jit(solution)/shard_map/ppermute | solution.py:35
  377.4 17.1 %collective-permute-start.62 = (bf16[64,2048]{1,0:T(8,128)(2,1)}, bf16[64,2048]{1,0:T(8,128)(2,1)}, u32[]{:S(2)}, u32[]{:S(2)}) collective-permute-start(bf16[64,2048]{1,0:T(8,128)(2,1)} %get-tuple-element.251), channel_id=1, source_target_pairs={{0,2},{2,0},{1,3},{3,1},{4,6},{6,4},{5,7},{7,5},{8,10},{10,8},{9,1... | collective-permute-start | bytes 786440 | tf_op jit(solution)/shard_map/ppermute | solution.py:31
  377.4 17.1 %collective-permute-start.63 = (bf16[64,2048]{1,0:T(8,128)(2,1)}, bf16[64,2048]{1,0:T(8,128)(2,1)}, u32[]{:S(2)}, u32[]{:S(2)}) collective-permute-start(bf16[64,2048]{1,0:T(8,128)(2,1)} %get-tuple-element.253), channel_id=1, source_target_pairs={{0,64},{64,0},{1,65},{65,1},{2,66},{66,2},{3,67},{67,3},{4,68},{68... | collective-permute-start | bytes 786440 | tf_op jit(solution)/shard_map/ppermute | solution.py:31
  378.5 16.2 %collective-permute-start.64 = (bf16[64,2048]{1,0:T(8,128)(2,1)S(1)}, bf16[64,2048]{1,0:T(8,128)(2,1)}, u32[]{:S(2)}, u32[]{:S(2)}) collective-permute-start(bf16[64,2048]{1,0:T(8,128)(2,1)S(1)} %get-tuple-element.252), channel_id=1, source_target_pairs={{0,66},{2,64},{64,2},{66,0},{1,67},{3,65},{65,3},{67,1},{4,70},{6,... | collective-permute-start | bytes 786440 | tf_op jit(solution)/shard_map/ppermute | solution.py:35
  396.2 8.8 %collective-permute-start.65 = (bf16[64,2048]{1,0:T(8,128)(2,1)S(1)}, bf16[64,2048]{1,0:T(8,128)(2,1)S(1)}, u32[]{:S(2)}, u32[]{:S(2)}) collective-permute-start(bf16[64,2048]{1,0:T(8,128)(2,1)S(1)} %fusion.42), channel_id=1, source_target_pairs={{0,2},{2,0},{1,3},{3,1},{4,6},{6,4},{5,7},{7,5},{8,10},{10,8},{9,1... | collective-permute-start | bytes 786440 | tf_op jit(solution)/shard_map/ppermute | solution.py:31
  400.0 13.4 %collective-permute-start.69 = (bf16[64,2304]{1,0:T(8,128)(2,1)S(1)}, bf16[64,2304]{1,0:T(8,128)(2,1)S(1)}, u32[]{:S(2)}, u32[]{:S(2)}) collective-permute-start(bf16[64,2304]{1,0:T(8,128)(2,1)S(1)} %get-tuple-element.201), channel_id=1, source_target_pairs={{0,64},{64,0},{1,65},{65,1},{2,66},{66,2},{3,67},{67,3},{4,68},{68... | collective-permute-start | bytes 884744 | tf_op jit(solution)/shard_map/ppermute | solution.py:31
  424.4 9.2 %collective-permute-start.73 = (bf16[64,1152]{1,0:T(8,128)(2,1)S(1)}, bf16[64,1152]{1,0:T(8,128)(2,1)S(1)}, u32[]{:S(2)}, u32[]{:S(2)}) collective-permute-start(bf16[64,1152]{1,0:T(8,128)(2,1)S(1)} %fusion.64), channel_id=1, source_target_pairs={{0,64},{64,0},{1,65},{65,1},{2,66},{66,2},{3,67},{67,3},{4,68},{68... | collective-permute-start | bytes 442376 | tf_op jit(solution)/shard_map/ppermute | solution.py:31
  428.4 12.1 %collective-permute-start.71 = (bf16[64,2048]{1,0:T(8,128)(2,1)S(1)}, bf16[64,2048]{1,0:T(8,128)(2,1)S(1)}, u32[]{:S(2)}, u32[]{:S(2)}) collective-permute-start(bf16[64,2048]{1,0:T(8,128)(2,1)S(1)} %reduce-precision_convert_fusion), channel_id=1, source_target_pairs={{0,2},{2,0},{1,3},{3,1},{4,6},{6,4},{5,7},{7,5},{8,10},{10,8},{9,1... | collective-permute-start | bytes 786440 | tf_op jit(solution)/shard_map/ppermute | solution.py:31
  428.9 12.1 %collective-permute-start.70 = (bf16[128,2048]{1,0:T(8,128)(2,1)}, bf16[128,2048]{1,0:T(8,128)(2,1)}, u32[]{:S(2)}, u32[]{:S(2)}) collective-permute-start(bf16[128,2048]{1,0:T(8,128)(2,1)} %pad_maximum_fusion.9), channel_id=1, source_target_pairs={{0,1},{1,0},{2,3},{3,2},{4,5},{5,4},{6,7},{7,6},{8,9},{9,8},{10,11... | collective-permute-start | bytes 1572872 | tf_op jit(solution)/shard_map/ppermute | solution.py:31
  (91 other events, 897.0 us)
Sparse Core Ops, SparseCore 0:
  26.3 55.2 all-gather.2
  83.7 90.1 all-gather.4
  233.6 104.3 reduce-scatter.9
  342.4 51.9 reduce-scatter.5
  396.8 22.6 reduce-scatter.7
where the time goes:
time: 458 us; the launch traced here: 453 us
  starting transfers between devices  159 us (35%)
  waiting for transfers between devices  130 us (28%)
  Pallas kernels  42.7 us (9%)
  other arithmetic  40.9 us (9%)
  local copies, waits for them, and re-layouts  34 us (7%)
  matrix products  30.5 us (7%)
  between operations  15.6 us (3%)
    ppermute x30, starting transfers between devices, swap(): return lax.ppermute(value, axis, [(0, 1), (1, 0)])  72.9 us
    ppermute x40, starting transfers between devices, shift(): return lax.ppermute(value, axis, [(i, (i + step) % 4) for i in range(4)])  69.1 us
    ppermute x40, waiting for transfers between devices, shift(): return lax.ppermute(value, axis, [(i, (i + step) % 4) for i in range(4)])  59.2 us
    ppermute x30, waiting for transfers between devices, swap(): return lax.ppermute(value, axis, [(0, 1), (1, 0)])  43.4 us
    dot_general x10, matrix products, dot_nt(): lax.dot_general(left, right, (((1,), (1,)), ((), ())), preferred_element_...  20.5 us
    unnamed x156, local copies, waits for them, and re-layouts  18.6 us
    pallas_call x3, Pallas kernels, plane_grads(): pl.pallas_call(kernel, grid=(count,), in_specs=[pl.BlockSpec((depth, heig...  18.5 us
    ppermute x6, starting transfers between devices, swap_both(): return lax.ppermute(value, ('zh', 'zl'), [(0, 3), (1, 2), (2, 1), (3, 0)])  11.9 us
  transfers between devices with their start and end apart: 83, of which 39 were waited for; matrix products, arithmetic and copies ran while one was open for 14% of the time, Pallas kernels for 9%

commit v1 on v0

--- a/solution.py
+++ b/solution.py
@@ -75,7 +75,6 @@
         ]
         return pieces, later
     next_to = [(shift(line, axis, -1), shift(line, axis, 1)) for line, axis in zip(lines, ("y", "x"))]
-    next_to = lax.optimization_barrier(next_to)
     return [
         [line, up, shift(up[:2], axis, -1), shift(down[2:], axis, 1), down]
         for line, (up, down), axis in zip(lines, next_to, ("y", "x"))
@@ -446,6 +445,38 @@
         cost_estimate=pl.CostEstimate(flops=0, bytes_accessed=4 * 2**20, transcendentals=0),
         name="arrange",
     )(info, own, other)
+
+
+def pack(side, key, value, query, gate, out, gains):
+    shards = [key, value, query, gate, out]
+
+    def kernel(side_ref, gains, *refs):
+        (own, sent), held, sems = refs[5:7], refs[7:12], refs[12]
+        for copy in bring(list(zip(refs[:5], held)), sems):
+            copy.wait()
+        key, value, query, gate, out = held
+        for target, zh in ((own, side_ref[0]), (sent, 1 - side_ref[0])):
+            narrow = pl.ds(pl.multiple_of(zh * HD, HD), HD)
+            wide = pl.ds(pl.multiple_of(zh * 2 * HD, HD), 2 * HD)
+            target[:, 0:HD] = key[:, narrow]
+            target[:, HD : 2 * HD] = gains[:, 0:HD]
+            target[:, 2 * HD : 3 * HD] = value[:, narrow]
+            target[:, 3 * HD : 4 * HD] = gains[:, HD : 2 * HD]
+            target[:, 4 * HD : 6 * HD] = query[:, wide]
+            target[:, 6 * HD : 8 * HD] = gate[:, wide]
+            target[:, 8 * HD : 10 * HD] = out[:, wide]
+
+    return pl.pallas_call(
+        kernel,
+        out_shape=(shaped(bfloat, 64, 10 * HD), shaped(bfloat, 64, 10 * HD)),
+        in_specs=[SMEM, VMEM] + [HBM] * 5,
+        out_specs=(VMEM, VMEM),
+        scratch_shapes=[pltpu.VMEM(shard.shape, bfloat) for shard in shards]
+        + [pltpu.SemaphoreType.DMA((5,))],
+        compiler_params=pltpu.CompilerParams(vmem_limit_bytes=4 * 2**20),
+        cost_estimate=pl.CostEstimate(flops=0, bytes_accessed=2**20, transcendentals=0),
+        name="pack",
+    )(side, gains, *in_hbm(shards))
 
 
 def project_pairs(info, own, other, cosine, sine, pieces):
@@ -702,27 +733,6 @@
         jnp.stack([head_gain(query_gain), head_gain(key_gain)], axis=0), ((0, 62), (0, 0))
     ).astype(bfloat)
 
-    def pairs_pack(side):
-        return jnp.concatenate(
-            [
-                columns_of(key_weight, side, HD),
-                norm_columns,
-                columns_of(value_weight, side, HD),
-                head_rows,
-            ],
-            axis=1,
-        )
-
-    def outer_pack(side):
-        return jnp.concatenate(
-            [
-                columns_of(query_weight, side, 256),
-                columns_of(gate_weight, side, 256),
-                rows_of(out_weight, side, 256).T,
-            ],
-            axis=1,
-        )
-
     def inner_pack(side):
         gate, lift, down = inner_shards
         return jnp.concatenate(
@@ -735,9 +745,17 @@
         other = swap(pack(1 - zh), "zh")
         return in_order(zh, own[None], other[None], 0)
 
-    first_block = pair_up(
-        lambda side: jnp.concatenate([pairs_pack(side), outer_pack(side)], axis=1)
-    )
+    own_pack, sent_pack = pack(
+        zh.astype(jnp.int32).reshape(1),
+        key_weight,
+        value_weight,
+        query_weight,
+        gate_weight,
+        out_weight.T,
+        jnp.concatenate([norm_columns, head_rows], axis=1),
+    )
+    first_block = in_order(zh, own_pack[None], swap(sent_pack, "zh")[None], 0)
+
     index = jnp.arange(512, dtype=jnp.int32)
     half_of = (index >> 7) & 1
     place = jnp.where(half_of == 0, block_own, block_other) * BLOCK + row_place(

time: 458 us -> 452 us (0.987)
  waiting for transfers between devices: 130 us -> 120 us
  starting transfers between devices: 159 us -> 166 us
  local copies, waits for them, and re-layouts: 34 us -> 29.4 us
    ppermute x40, starting transfers between devices: 69.1 us -> 83.2 us  [shift(): return lax.ppermute(value, axis, [(i, (i + step) % 4) for i in range(4)])]
    ppermute x40, waiting for transfers between devices: 59.2 us -> 48.8 us  [shift(): return lax.ppermute(value, axis, [(i, (i + step) % 4) for i in range(4)])]
    ppermute x30, starting transfers between devices: 72.9 us -> 66.1 us  [swap(): return lax.ppermute(value, axis, [(0, 1), (1, 0)])]
    unnamed x156 -> x146, local copies, waits for them, and re-layouts: 18.6 us -> 14.7 us
  transfers between devices with their start and end apart: 83 -> 83, of which waited for: 39 -> 39; matrix products, arithmetic and copies ran while one was open for 14% -> 14% of each run, Pallas kernels for 9% -> 10%
where the time goes in v1:
time: 452 us; the launch traced here: 445 us
  starting transfers between devices  166 us (37%)
  waiting for transfers between devices  120 us (27%)
  Pallas kernels  43.5 us (10%)
  other arithmetic  39.8 us (9%)
  matrix products  30.4 us (7%)
  local copies, waits for them, and re-layouts  29.4 us (7%)
  between operations  15.6 us (3%)
    ppermute x40, starting transfers between devices, shift(): return lax.ppermute(value, axis, [(i, (i + step) % 4) for i in range(4)])  83.2 us
    ppermute x30, starting transfers between devices, swap(): return lax.ppermute(value, axis, [(0, 1), (1, 0)])  66.1 us
    ppermute x40, waiting for transfers between devices, shift(): return lax.ppermute(value, axis, [(i, (i + step) % 4) for i in range(4)])  48.8 us
    ppermute x30, waiting for transfers between devices, swap(): return lax.ppermute(value, axis, [(0, 1), (1, 0)])  42.6 us
    dot_general x10, matrix products, dot_nt(): lax.dot_general(left, right, (((1,), (1,)), ((), ())), preferred_element_...  20.4 us
    pallas_call x3, Pallas kernels, plane_grads(): pl.pallas_call(kernel, grid=(count,), in_specs=[pl.BlockSpec((depth, heig...  18.5 us
    unnamed x146, local copies, waits for them, and re-layouts  14.7 us
    ppermute x6, waiting for transfers between devices, swap_both(): return lax.ppermute(value, ('zh', 'zl'), [(0, 3), (1, 2), (2, 1), (3, 0)])  12.2 us
  transfers between devices with their start and end apart: 83, of which 39 were waited for; matrix products, arithmetic and copies ran while one was open for 14% of the time, Pallas kernels for 10%

profile of v1, /device:TPU:1, one launch (start us, length us, event | category | flops | bytes accessed | tf_op | source)
XLA Modules:
  0.0 444.6 jit_solution(1171263699903955610)
XLA Ops:
  10.7 4.5 %collective-permute-start = (bf16[64,1280]{1,0:T(8,128)(2,1)S(1)}, bf16[64,1280]{1,0:T(8,128)(2,1)S(1)}, u32[]{:S(2)}, u32[]{:S(2)}) collective-permute-start(bf16[64,1280]{1,0:T(8,128)(2,1)S(1)} %get-tuple-element.111), channel_id=1, source_target_pairs={{0,64},{64,0},{1,65},{65,1},{2,66},{66,2},{3,67},{67,3},{4,68},{68... | collective-permute-start | bytes 491528 | tf_op jit(solution)/shard_map/ppermute | solution.py:31
  19.5 2.7 stack.101.info
  23.6 2.5 collective-permute-start.2
  27.3 2.7 collective-permute-start.5
  32.5 2.6 collective-permute-done.6
  36.0 2.2 collective-permute-start.11
  39.3 5.9 %collective-permute-done.11.refs_7_ = bf16[4,128,256]{2,1,0:T(8,128)(2,1)S(1)} collective-permute-done((bf16[4,128,256]{2,1,0:T(8,128)(2,1)S(1)}, bf16[4,128,256]{2,1,0:T(8,128)(2,1)S(1)}, u32[]{:S(2)}, u32[]{:S(2)}) %collective-permute-start.11) | collective-permute-done | bytes 262176 | tf_op jit(solution)/shard_map/ppermute | solution.py:61
  47.7 6.5 %collective-permute-done.13.refs_9_ = bf16[4,128,256]{2,1,0:T(8,128)(2,1)S(1)} collective-permute-done((bf16[4,128,256]{2,1,0:T(8,128)(2,1)S(1)}, bf16[4,128,256]{2,1,0:T(8,128)(2,1)S(1)}, u32[]{:S(2)}, u32[]{:S(2)}) %collective-permute-start.13) | collective-permute-done | bytes 262176 | tf_op jit(solution)/shard_map/ppermute | solution.py:61
  54.9 4.8 %project_pairs.1 = (bf16[512,2048]{1,0:T(8,128)(2,1)S(1)}, bf16[512,128]{1,0:T(8,128)(2,1)S(1)}, bf16[512,128]{1,0:T(8,128)(2,1)S(1)}, f32[512,128]{1,0:T(8,128)...) custom-call(s32[10]{0:T(128)S(1)} %stack.101.info, ...), custom_call_target="tpu_custom_call" | custom-call | flops 1073741824 | bytes 8388608 | tf_op jit(solution)/shard_map/project_pairs/pallas_call | solution.py:484
  60.9 2.9 collective-permute-start.20
  63.8 3.4 collective-permute-start.14
  68.9 3.8 collective-permute-start.17
  82.4 2.9 collective-permute-start.26
  86.4 2.3 collective-permute-start.22
  88.8 2.7 collective-permute-done.26.refs_7_.refs_12_
  92.3 3.1 collective-permute-start.27
  96.9 2.3 collective-permute-start.23
  100.1 3.1 arrange.1.refs_1_
  108.6 6.0 %collective-permute-done.25.refs_4_.refs_9_ = bf16[2,512,128]{2,1,0:T(8,128)(2,1)} collective-permute-done((bf16[2,512,128]{2,1,0:T(8,128)(2,1)}, bf16[2,512,128]{2,1,0:T(8,128)(2,1)}, u32[]{:S(2)}, u32[]{:S(2)}) %collective-permute-start.25) | collective-permute-done | bytes 262176 | tf_op jit(solution)/shard_map/ppermute | solution.py:61
  114.6 5.0 %attend.1 = (f32[512,256]{1,0:T(8,128)S(1)}, f32[2,1,512]{2,1,0:T(1,128)S(1)}) custom-call(s32[10]{0:T(128)S(1)} %copy-done.25, s32[32]{0:T(128)S(1)} %copy-done.26, bf16[512,256]{1,0:T(8,128)(2,1)} %copy-done.28, bf16[4,512,128]{2,1,0:T(8,128)(2,1)} %copy-done.49, bf16[4,512,128]{2,1,0:T(8,128)(2,1)} %copy-done.60, ...), custom_call_target="tpu_custom_call" | custom-call | flops 4294967296 | bytes 6291456 | tf_op jit(solution)/shard_map/attend/pallas_call | solution.py:531
  122.7 17.8 %collective-permute-start.30 = (bf16[256,2048]{1,0:T(8,128)(2,1)}, bf16[256,2048]{1,0:T(8,128)(2,1)}, u32[]{:S(2)}, u32[]{:S(2)}) collective-permute-start(bf16[256,2048]{1,0:T(8,128)(2,1)} %convolution_convert_fusion), channel_id=1, source_target_pairs={{0,1},{1,0},{2,3},{3,2},{4,5},{5,4},{6,7},{7,6},{8,9},{9,8},{10,11... | collective-permute-start | bytes 3145736 | tf_op jit(solution)/shard_map/ppermute | solution.py:31
  140.5 2.6 collective-permute-done.30
  145.2 3.8 collective-permute-start.33
  148.9 3.8 collective-permute-done.31
  152.7 4.1 collective-permute-done.32
  156.8 3.6 collective-permute-done.33
  163.4 3.5 collective-permute-start.35
  167.2 2.6 collective-permute-done.34
  169.8 7.3 %collective-permute-done.35 = bf16[64,2048]{1,0:T(8,128)(2,1)S(1)} collective-permute-done((bf16[64,2048]{1,0:T(8,128)(2,1)S(1)}, bf16[64,2048]{1,0:T(8,128)(2,1)S(1)}, u32[]{:S(2)}, u32[]{:S(2)}) %collective-permute-start.35) | collective-permute-done | bytes 262176 | tf_op jit(solution)/shard_map/ppermute | solution.py:31
  177.1 3.1 collective-permute-done.36
  180.3 2.7 collective-permute-start.37
  186.3 6.3 %fusion.4 = f32[512,1536]{1,0:T(8,128)S(1)} fusion(bf16[512,2048]{1,0:T(8,128)(2,1)} %constant_dynamic-update-slice_fusion.refs_0_, bf16[2048,2304]{1,0:T(8,128)(2,1)} %bitcast.152), kind=kOutput, calls=%fused_computation.4 | convolution fusion | flops 3221225472 | bytes 11534336 | tf_op jit(solution)/shard_map/dot_general | solution.py:809
  193.1 2.3 multiply_convert_fusion.2
  197.7 2.3 collective-permute-done.38
  204.9 2.3 collective-permute-start.41
  207.2 12.2 %plane_grads.3 = bf16[16,128,2304]{2,1,0:T(8,128)(2,1)} custom-call(bf16[512,2048]{1,0:T(8,128)(2,1)} %constant_dynamic-update-slice_fusion.refs_0_, bf16[512,2048]{1,0:T(8,128)(2,1)S(1)} %copy-done.11, bf16[512,768]{1,0:T(8,128)(2,1)S(1)} %get-tuple-element.146.refs_2_, bf16[512,768]{1,0:T(8,128)(2,1)S(1)} %get-tuple-element.147.refs_3_, ...), custom_call_target="tpu_custom_call" | custom-call | flops 4831838208 | bytes 13893632 | tf_op jit(solution)/shard_map/plane_grads/pallas_call | solution.py:639
  221.3 2.4 constant_dynamic-update-slice_fusion.9
  223.7 3.0 collective-permute-start.43
  227.7 2.4 collective-permute-done.42
  230.1 6.7 %collective-permute-done.43 = bf16[64,2048]{1,0:T(8,128)(2,1)S(1)} collective-permute-done((bf16[64,2048]{1,0:T(8,128)(2,1)S(1)}, bf16[64,2048]{1,0:T(8,128)(2,1)S(1)}, u32[]{:S(2)}, u32[]{:S(2)}) %collective-permute-start.43) | collective-permute-done | bytes 262176 | tf_op jit(solution)/shard_map/ppermute | solution.py:31
  236.8 3.5 collective-permute-done.44
  242.7 2.2 collective-permute-done.45
  246.5 8.8 %attend_back.1 = (bf16[512,256]{1,0:T(8,128)(2,1)S(1)}, f32[1,128]{1,0:T(1,128)S(1)}, bf16[4,512,128]{2,1,0:T(8,128)(2,1)}, bf16[4,512,128]{2,1,0:T(8,128)(2,1)}...) custom-call(s32[10]{0:T(128)S(1)} %copy-done.25, ...), custom_call_target="tpu_custom_call" | custom-call | flops 10737418240 | bytes 12582912 | tf_op jit(solution)/shard_map/attend_back/pallas_call | solution.py:554
  257.2 28.4 %collective-permute-start.47 = (bf16[2,512,128]{2,1,0:T(8,128)(2,1)}, bf16[2,512,128]{2,1,0:T(8,128)(2,1)S(1)}, u32[]{:S(2)}, u32[]{:S(2)}) collective-permute-start(bf16[2,512,128]{2,1,0:T(8,128)(2,1)} %get-tuple-element.156), channel_id=1, source_target_pairs={{0,12},{4,0},{8,4},{12,8},{1,13},{5,1},{9,5},{13,9},{2,14},{6,2},{... | collective-permute-start | bytes 786440 | tf_op jit(solution)/shard_map/ppermute | solution.py:61
  285.6 2.9 collective-permute-start.49
  288.7 4.5 %plane_grads.4 = bf16[16,128,768]{2,1,0:T(8,128)(2,1)} custom-call(bf16[512,2048]{1,0:T(8,128)(2,1)S(1)} %constant_dynamic-update-slice_fusion.5.refs_0_, bf16[512,2048]{1,0:T(8,128)(2,1)S(1)} %copy-done.3, bf16[512,256]{1,0:T(8,128)(2,1)S(1)} %copy-done.13, bf16[512,256]{1,0:T(8,128)(2,1)S(1)} %get-tuple-element.250.refs_3_, ...), custom_call_target="tpu_custom_call" | custom-call | flops 1610612736 | bytes 6029312 | tf_op jit(solution)/shard_map/plane_grads/pallas_call | solution.py:639
  293.2 4.5 %collective-permute-done.46.refs_1_ = bf16[2,512,128]{2,1,0:T(8,128)(2,1)S(1)} collective-permute-done((bf16[2,512,128]{2,1,0:T(8,128)(2,1)}, bf16[2,512,128]{2,1,0:T(8,128)(2,1)S(1)}, u32[]{:S(2)}, u32[]{:S(2)}) %collective-permute-start.46) | collective-permute-done | bytes 262176 | tf_op jit(solution)/shard_map/ppermute | solution.py:61
  299.2 2.7 collective-permute-start.51
  301.9 2.7 collective-permute-start.53
  306.6 6.4 %collective-permute-done.50 = bf16[4,512,128]{2,1,0:T(8,128)(2,1)S(1)} collective-permute-done((bf16[4,512,128]{2,1,0:T(8,128)(2,1)S(1)}, bf16[4,512,128]{2,1,0:T(8,128)(2,1)S(1)}, u32[]{:S(2)}, u32[]{:S(2)}) %collective-permute-start.50) | collective-permute-done | bytes 524320 | tf_op jit(solution)/shard_map/ppermute | solution.py:61
  314.2 3.0 collective-permute-done.52
  322.7 4.7 %collective-permute-start.55 = (bf16[512,128]{1,0:T(8,128)(2,1)S(1)}, bf16[512,128]{1,0:T(8,128)(2,1)S(1)}, u32[]{:S(2)}, u32[]{:S(2)}) collective-permute-start(bf16[512,128]{1,0:T(8,128)(2,1)S(1)} %get-tuple-element.276), channel_id=1, source_target_pairs={{0,32},{16,48},{32,0},{48,16},{1,33},{17,49},{33,1},{49,17},{2,34}... | collective-permute-start | bytes 393224 | tf_op jit(solution)/shard_map/ppermute | solution.py:61
  329.0 2.5 collective-permute-start.56
  338.8 7.5 %collective-permute-start.60 = (bf16[256,2048]{1,0:T(8,128)(2,1)S(1)}, bf16[256,2048]{1,0:T(8,128)(2,1)S(1)}, u32[]{:S(2)}, u32[]{:S(2)}) collective-permute-start(bf16[256,2048]{1,0:T(8,128)(2,1)S(1)} %add_convert_fusion), channel_id=1, source_target_pairs={{0,1},{1,0},{2,3},{3,2},{4,5},{5,4},{6,7},{7,6},{8,9},{9,8},{10,11... | collective-permute-start | bytes 3145736 | tf_op jit(solution)/shard_map/ppermute | solution.py:31
  350.2 3.9 convolution_convert_fusion.1
  355.4 4.9 %all-to-all-start = ((bf16[16,144,256]{2,1,0:T(8,128)(2,1)}), bf16[16,144,256]{2,1,0:T(8,128)(2,1)}, u32[]{:S(2)}, u32[]{:S(2)}) async-start(bf16[16,144,256]{2,1,0:T(8,128)(2,1)} %plane_grads.5), calls=%async_computation | async-start | bytes 2359296 | tf_op jit(solution)/shard_map/all_to_all | solution.py:893
  364.5 4.5 %fusion.117 = (bf16[256,2048]{1,0:T(8,128)(2,1)S(1)}, f32[256,2048]{1,0:T(8,128)}) fusion(bf16[256,2048]{1,0:T(8,128)(2,1)} %collective-permute-done.61, bf16[2048,2304]{1,0:T(8,128)(2,1)} %bitcast.154, bf16[512,768]{1,0:T(8,128)(2,1)S(1)} %copy-done.23), kind=kOutput, calls=%fused_computation.270 | convolution fusion | flops 806879232 | bytes 7733248 | tf_op jit(solution)/shard_map/dot_general | solution.py:240
  377.7 9.8 %reduce-scatter.6.cloned.1.call-done = bf16[1,4,128,768]{3,2,1,0:T(8,128)(2,1)} async-done(((bf16[4,4,128,768]{3,2,1,0:T(8,128)(2,1)}), bf16[1,4,128,768]{3,2,1,0:T(8,128)(2,1)}) %reduce-scatter.6.cloned.1.call-update) | async-done | bytes 786448 | tf_op jit(solution)/shard_map/reduce_scatter | solution.py:877
  389.1 2.9 collective-permute-start.65
  393.2 2.4 collective-permute-start.69
  399.0 7.4 %collective-permute-done.69 = bf16[64,2304]{1,0:T(8,128)(2,1)S(1)} collective-permute-done((bf16[64,2304]{1,0:T(8,128)(2,1)S(1)}, bf16[64,2304]{1,0:T(8,128)(2,1)S(1)}, u32[]{:S(2)}, u32[]{:S(2)}) %collective-permute-start.69) | collective-permute-done | bytes 294944 | tf_op jit(solution)/shard_map/ppermute | solution.py:31
  406.4 6.2 %reduce-scatter.8.cloned.1.call-done = bf16[1,128,768]{2,1,0:T(8,128)(2,1)} async-done(((bf16[4,128,768]{2,1,0:T(8,128)(2,1)}), bf16[1,128,768]{2,1,0:T(8,128)(2,1)}) %reduce-scatter.8.cloned.1.call-update) | async-done | bytes 196624 | tf_op jit(solution)/shard_map/reduce_scatter | solution.py:880
  417.6 3.0 collective-permute-start.73
  422.1 2.2 collective-permute-start.70
  (398 shorter events, 130.7 us)
Async XLA Ops:
  7.2 96.1 %all-gather.3.cloned.1.call-start = ((), (), s32[]{:S(2)}) async-start(), calls=%async_computation.4 | async-start | bytes 3342336 | tf_op jit(solution)/shard_map/all_gather | solution.py:680
  10.7 11.7 %collective-permute-start = (bf16[64,1280]{1,0:T(8,128)(2,1)S(1)}, bf16[64,1280]{1,0:T(8,128)(2,1)S(1)}, u32[]{:S(2)}, u32[]{:S(2)}) collective-permute-start(bf16[64,1280]{1,0:T(8,128)(2,1)S(1)} %get-tuple-element.111), channel_id=1, source_target_pairs={{0,64},{64,0},{1,65},{65,1},{2,66},{66,2},{3,67},{67,3},{4,68},{68... | collective-permute-start | bytes 491528 | tf_op jit(solution)/shard_map/ppermute | solution.py:31
  23.3 162.9 %all-gather.5.cloned.1.call-start = ((), (), s32[]{:S(2)}) async-start(), calls=%async_computation.5 | async-start | bytes 10027008 | tf_op jit(solution)/shard_map/all_gather | solution.py:680
  23.4 31.5 %collective-permute-start.1 = (bf16[256,2048]{1,0:T(8,128)(2,1)S(1)}, bf16[256,2048]{1,0:T(8,128)(2,1)}, u32[]{:S(2)}, u32[]{:S(2)}) collective-permute-start(bf16[256,2048]{1,0:T(8,128)(2,1)S(1)} %copy-done.36), channel_id=1, source_target_pairs={{0,64},{64,0},{1,65},{65,1},{2,66},{66,2},{3,67},{67,3},{4,68},{68... | collective-permute-start | bytes 3145736 | tf_op jit(solution)/shard_map/ppermute | solution.py:31
  36.0 9.2 %collective-permute-start.11 = (bf16[4,128,256]{2,1,0:T(8,128)(2,1)S(1)}, bf16[4,128,256]{2,1,0:T(8,128)(2,1)S(1)}, u32[]{:S(2)}, u32[]{:S(2)}) collective-permute-start(bf16[4,128,256]{2,1,0:T(8,128)(2,1)S(1)} %pad_maximum_fusion.22.refs_6_), channel_id=1, source_target_pairs={{0,12},{4,0},{8,4},{12,8},{1,13},{5,1},{9,5},{13,9},{2,14},{6,2},{... | collective-permute-start | bytes 786440 | tf_op jit(solution)/shard_map/ppermute | solution.py:61
  38.2 8.3 %collective-permute-start.12 = (bf16[4,128,256]{2,1,0:T(8,128)(2,1)S(1)}, bf16[4,128,256]{2,1,0:T(8,128)(2,1)S(1)}, u32[]{:S(2)}, u32[]{:S(2)}) collective-permute-start(bf16[4,128,256]{2,1,0:T(8,128)(2,1)S(1)} %pad_maximum_fusion.22.refs_6_), channel_id=1, source_target_pairs={{0,8},{4,12},{8,0},{12,4},{1,9},{5,13},{9,1},{13,5},{2,10},{6,14},... | collective-permute-start | bytes 786440 | tf_op jit(solution)/shard_map/ppermute | solution.py:61
  39.2 15.0 %collective-permute-start.13 = (bf16[4,128,256]{2,1,0:T(8,128)(2,1)S(1)}, bf16[4,128,256]{2,1,0:T(8,128)(2,1)S(1)}, u32[]{:S(2)}, u32[]{:S(2)}) collective-permute-start(bf16[4,128,256]{2,1,0:T(8,128)(2,1)S(1)} %pad_maximum_fusion.22.refs_6_), channel_id=1, source_target_pairs={{0,4},{4,8},{8,12},{12,0},{1,5},{5,9},{9,13},{13,1},{2,6},{6,10},{... | collective-permute-start | bytes 786440 | tf_op jit(solution)/shard_map/ppermute | solution.py:61
  39.2 15.0 %collective-permute-start.10 = (bf16[4,128,256]{2,1,0:T(8,128)(2,1)S(1)}, bf16[4,128,256]{2,1,0:T(8,128)(2,1)}, u32[]{:S(2)}, u32[]{:S(2)}) collective-permute-start(bf16[4,128,256]{2,1,0:T(8,128)(2,1)S(1)} %pad_maximum_fusion.21.refs_2_), channel_id=1, source_target_pairs={{0,16},{16,32},{32,48},{48,0},{1,17},{17,33},{33,49},{49,1},{2,18}... | collective-permute-start | bytes 786440 | tf_op jit(solution)/shard_map/ppermute | solution.py:61
  45.2 9.0 %collective-permute-start.8 = (bf16[4,128,256]{2,1,0:T(8,128)(2,1)S(1)}, bf16[4,128,256]{2,1,0:T(8,128)(2,1)}, u32[]{:S(2)}, u32[]{:S(2)}) collective-permute-start(bf16[4,128,256]{2,1,0:T(8,128)(2,1)S(1)} %pad_maximum_fusion.21.refs_2_), channel_id=1, source_target_pairs={{0,48},{16,0},{32,16},{48,32},{1,49},{17,1},{33,17},{49,33},{2,50}... | collective-permute-start | bytes 786440 | tf_op jit(solution)/shard_map/ppermute | solution.py:61
  60.9 11.8 %collective-permute-start.20 = (bf16[64,2304]{1,0:T(8,128)(2,1)S(1)}, bf16[64,2304]{1,0:T(8,128)(2,1)S(1)}, u32[]{:S(2)}, u32[]{:S(2)}) collective-permute-start(bf16[64,2304]{1,0:T(8,128)(2,1)S(1)} %pad_maximum_fusion.16), channel_id=1, source_target_pairs={{0,64},{64,0},{1,65},{65,1},{2,66},{66,2},{3,67},{67,3},{4,68},{68... | collective-permute-start | bytes 884744 | tf_op jit(solution)/shard_map/ppermute | solution.py:31
  63.8 9.8 %collective-permute-start.14 = (bf16[512,128]{1,0:T(8,128)(2,1)S(1)}, bf16[512,128]{1,0:T(8,128)(2,1)S(1)}, u32[]{:S(2)}, u32[]{:S(2)}) collective-permute-start(bf16[512,128]{1,0:T(8,128)(2,1)S(1)} %get-tuple-element.126), channel_id=1, source_target_pairs={{0,12},{4,0},{8,4},{12,8},{1,13},{5,1},{9,5},{13,9},{2,14},{6,2},{... | collective-permute-start | bytes 393224 | tf_op jit(solution)/shard_map/ppermute | solution.py:61
  67.2 9.5 %collective-permute-start.15 = (bf16[512,128]{1,0:T(8,128)(2,1)S(1)}, bf16[512,128]{1,0:T(8,128)(2,1)}, u32[]{:S(2)}, u32[]{:S(2)}) collective-permute-start(bf16[512,128]{1,0:T(8,128)(2,1)S(1)} %get-tuple-element.126), channel_id=1, source_target_pairs={{0,8},{4,12},{8,0},{12,4},{1,9},{5,13},{9,1},{13,5},{2,10},{6,14},... | collective-permute-start | bytes 393224 | tf_op jit(solution)/shard_map/ppermute | solution.py:61
  68.9 8.8 %collective-permute-start.16 = (bf16[512,128]{1,0:T(8,128)(2,1)S(1)}, bf16[512,128]{1,0:T(8,128)(2,1)}, u32[]{:S(2)}, u32[]{:S(2)}) collective-permute-start(bf16[512,128]{1,0:T(8,128)(2,1)S(1)} %get-tuple-element.126), channel_id=1, source_target_pairs={{0,4},{4,8},{8,12},{12,0},{1,5},{5,9},{9,13},{13,1},{2,6},{6,10},{... | collective-permute-start | bytes 393224 | tf_op jit(solution)/shard_map/ppermute | solution.py:61
  68.9 8.8 %collective-permute-start.17 = (bf16[512,128]{1,0:T(8,128)(2,1)S(1)}, bf16[512,128]{1,0:T(8,128)(2,1)}, u32[]{:S(2)}, u32[]{:S(2)}) collective-permute-start(bf16[512,128]{1,0:T(8,128)(2,1)S(1)} %get-tuple-element.127), channel_id=1, source_target_pairs={{0,48},{16,0},{32,16},{48,32},{1,49},{17,1},{33,17},{49,33},{2,50}... | collective-permute-start | bytes 393224 | tf_op jit(solution)/shard_map/ppermute | solution.py:61
  79.9 254.5 %reduce-scatter.10.cloned.1.call-start = ((), (), s32[]{:S(2)}) async-start(), calls=%async_computation.8 | async-start | bytes 10027008
  79.9 20.2 %collective-permute-start.21 = (bf16[256,2048]{1,0:T(8,128)(2,1)}, bf16[256,2048]{1,0:T(8,128)(2,1)}, u32[]{:S(2)}, u32[]{:S(2)}) collective-permute-start(bf16[256,2048]{1,0:T(8,128)(2,1)} %own.1), channel_id=1, source_target_pairs={{0,64},{64,0},{1,65},{65,1},{2,66},{66,2},{3,67},{67,3},{4,68},{68... | collective-permute-start | bytes 3145736 | tf_op jit(solution)/shard_map/ppermute | solution.py:31
  82.4 9.1 %collective-permute-start.26 = (bf16[4,512,128]{2,1,0:T(8,128)(2,1)S(1)}, bf16[4,512,128]{2,1,0:T(8,128)(2,1)S(1)}, u32[]{:S(2)}, u32[]{:S(2)}) collective-permute-start(bf16[4,512,128]{2,1,0:T(8,128)(2,1)S(1)} %pad_maximum_fusion.8.refs_6_.refs_11_), channel_id=1, source_target_pairs={{0,12},{4,0},{8,4},{12,8},{1,13},{5,1},{9,5},{13,9},{2,14},{6,2},{... | collective-permute-start | bytes 1572872 | tf_op jit(solution)/shard_map/ppermute | solution.py:61
  85.4 10.0 %collective-permute-start.28 = (bf16[4,512,128]{2,1,0:T(8,128)(2,1)S(1)}, bf16[4,512,128]{2,1,0:T(8,128)(2,1)S(1)}, u32[]{:S(2)}, u32[]{:S(2)}) collective-permute-start(bf16[4,512,128]{2,1,0:T(8,128)(2,1)S(1)} %pad_maximum_fusion.8.refs_6_.refs_11_), channel_id=1, source_target_pairs={{0,4},{4,8},{8,12},{12,0},{1,5},{5,9},{9,13},{13,1},{2,6},{6,10},{... | collective-permute-start | bytes 1572872 | tf_op jit(solution)/shard_map/ppermute | solution.py:61
  86.4 9.7 %collective-permute-start.22 = (bf16[4,512,128]{2,1,0:T(8,128)(2,1)S(1)}, bf16[4,512,128]{2,1,0:T(8,128)(2,1)S(1)}, u32[]{:S(2)}, u32[]{:S(2)}) collective-permute-start(bf16[4,512,128]{2,1,0:T(8,128)(2,1)S(1)} %pad_maximum_fusion.7.refs_1_.refs_6_), channel_id=1, source_target_pairs={{0,48},{16,0},{32,16},{48,32},{1,49},{17,1},{33,17},{49,33},{2,50}... | collective-permute-start | bytes 1572872 | tf_op jit(solution)/shard_map/ppermute | solution.py:61
  88.8 10.4 %collective-permute-start.24 = (bf16[4,512,128]{2,1,0:T(8,128)(2,1)S(1)}, bf16[4,512,128]{2,1,0:T(8,128)(2,1)S(1)}, u32[]{:S(2)}, u32[]{:S(2)}) collective-permute-start(bf16[4,512,128]{2,1,0:T(8,128)(2,1)S(1)} %pad_maximum_fusion.7.refs_1_.refs_6_), channel_id=1, source_target_pairs={{0,16},{16,32},{32,48},{48,0},{1,17},{17,33},{33,49},{49,1},{2,18}... | collective-permute-start | bytes 1572872 | tf_op jit(solution)/shard_map/ppermute | solution.py:61
  92.3 15.6 %collective-permute-start.27 = (bf16[2,512,128]{2,1,0:T(8,128)(2,1)}, bf16[2,512,128]{2,1,0:T(8,128)(2,1)}, u32[]{:S(2)}, u32[]{:S(2)}) collective-permute-start(bf16[2,512,128]{2,1,0:T(8,128)(2,1)} %slice.393), channel_id=1, source_target_pairs={{0,12},{4,0},{8,4},{12,8},{1,13},{5,1},{9,5},{13,9},{2,14},{6,2},{... | collective-permute-start | bytes 786440 | tf_op jit(solution)/shard_map/ppermute | solution.py:61
  96.2 11.7 %collective-permute-start.29 = (bf16[2,512,128]{2,1,0:T(8,128)(2,1)}, bf16[2,512,128]{2,1,0:T(8,128)(2,1)}, u32[]{:S(2)}, u32[]{:S(2)}) collective-permute-start(bf16[2,512,128]{2,1,0:T(8,128)(2,1)} %slice.394), channel_id=1, source_target_pairs={{0,4},{4,8},{8,12},{12,0},{1,5},{5,9},{9,13},{13,1},{2,6},{6,10},{... | collective-permute-start | bytes 786440 | tf_op jit(solution)/shard_map/ppermute | solution.py:61
  96.9 11.7 %collective-permute-start.23 = (bf16[2,512,128]{2,1,0:T(8,128)(2,1)}, bf16[2,512,128]{2,1,0:T(8,128)(2,1)}, u32[]{:S(2)}, u32[]{:S(2)}) collective-permute-start(bf16[2,512,128]{2,1,0:T(8,128)(2,1)} %slice.391), channel_id=1, source_target_pairs={{0,48},{16,0},{32,16},{48,32},{1,49},{17,1},{33,17},{49,33},{2,50}... | collective-permute-start | bytes 786440 | tf_op jit(solution)/shard_map/ppermute | solution.py:61
  100.0 14.7 %collective-permute-start.25 = (bf16[2,512,128]{2,1,0:T(8,128)(2,1)}, bf16[2,512,128]{2,1,0:T(8,128)(2,1)}, u32[]{:S(2)}, u32[]{:S(2)}) collective-permute-start(bf16[2,512,128]{2,1,0:T(8,128)(2,1)} %slice.392), channel_id=1, source_target_pairs={{0,16},{16,32},{32,48},{48,0},{1,17},{17,33},{33,49},{49,1},{2,18}... | collective-permute-start | bytes 786440 | tf_op jit(solution)/shard_map/ppermute | solution.py:61
  122.7 20.5 %collective-permute-start.30 = (bf16[256,2048]{1,0:T(8,128)(2,1)}, bf16[256,2048]{1,0:T(8,128)(2,1)}, u32[]{:S(2)}, u32[]{:S(2)}) collective-permute-start(bf16[256,2048]{1,0:T(8,128)(2,1)} %convolution_convert_fusion), channel_id=1, source_target_pairs={{0,1},{1,0},{2,3},{3,2},{4,5},{5,4},{6,7},{7,6},{8,9},{9,8},{10,11... | collective-permute-start | bytes 3145736 | tf_op jit(solution)/shard_map/ppermute | solution.py:31
  145.0 7.7 %collective-permute-start.31 = (bf16[64,2048]{1,0:T(8,128)(2,1)S(1)}, bf16[64,2048]{1,0:T(8,128)(2,1)S(1)}, u32[]{:S(2)}, u32[]{:S(2)}) collective-permute-start(bf16[64,2048]{1,0:T(8,128)(2,1)S(1)} %get-tuple-element.255), channel_id=1, source_target_pairs={{0,2},{2,0},{1,3},{3,1},{4,6},{6,4},{5,7},{7,5},{8,10},{10,8},{9,1... | collective-permute-start | bytes 786440 | tf_op jit(solution)/shard_map/ppermute | solution.py:31
  145.1 11.7 %collective-permute-start.32 = (bf16[64,2048]{1,0:T(8,128)(2,1)S(1)}, bf16[64,2048]{1,0:T(8,128)(2,1)S(1)}, u32[]{:S(2)}, u32[]{:S(2)}) collective-permute-start(bf16[64,2048]{1,0:T(8,128)(2,1)S(1)} %get-tuple-element.257), channel_id=1, source_target_pairs={{0,64},{64,0},{1,65},{65,1},{2,66},{66,2},{3,67},{67,3},{4,68},{68... | collective-permute-start | bytes 786440 | tf_op jit(solution)/shard_map/ppermute | solution.py:31
  145.2 15.3 %collective-permute-start.33 = (bf16[64,2048]{1,0:T(8,128)(2,1)S(1)}, bf16[64,2048]{1,0:T(8,128)(2,1)S(1)}, u32[]{:S(2)}, u32[]{:S(2)}) collective-permute-start(bf16[64,2048]{1,0:T(8,128)(2,1)S(1)} %get-tuple-element.256), channel_id=1, source_target_pairs={{0,66},{2,64},{64,2},{66,0},{1,67},{3,65},{65,3},{67,1},{4,70},{6,... | collective-permute-start | bytes 786440 | tf_op jit(solution)/shard_map/ppermute | solution.py:35
  163.4 13.7 %collective-permute-start.35 = (bf16[64,2048]{1,0:T(8,128)(2,1)S(1)}, bf16[64,2048]{1,0:T(8,128)(2,1)S(1)}, u32[]{:S(2)}, u32[]{:S(2)}) collective-permute-start(bf16[64,2048]{1,0:T(8,128)(2,1)S(1)} %get-tuple-element.223), channel_id=1, source_target_pairs={{0,64},{64,0},{1,65},{65,1},{2,66},{66,2},{3,67},{67,3},{4,68},{68... | collective-permute-start | bytes 786440 | tf_op jit(solution)/shard_map/ppermute | solution.py:31
  166.8 13.4 %collective-permute-start.36 = (bf16[64,2048]{1,0:T(8,128)(2,1)S(1)}, bf16[64,2048]{1,0:T(8,128)(2,1)S(1)}, u32[]{:S(2)}, u32[]{:S(2)}) collective-permute-start(bf16[64,2048]{1,0:T(8,128)(2,1)S(1)} %get-tuple-element.223), channel_id=1, source_target_pairs={{0,66},{2,64},{64,2},{66,0},{1,67},{3,65},{65,3},{67,1},{4,70},{6,... | collective-permute-start | bytes 786440 | tf_op jit(solution)/shard_map/ppermute | solution.py:35
  203.4 16.0 %collective-permute-start.39 = (bf16[64,2048]{1,0:T(8,128)(2,1)}, bf16[64,2048]{1,0:T(8,128)(2,1)}, u32[]{:S(2)}, u32[]{:S(2)}) collective-permute-start(bf16[64,2048]{1,0:T(8,128)(2,1)} %get-tuple-element.254), channel_id=1, source_target_pairs={{0,2},{2,0},{1,3},{3,1},{4,6},{6,4},{5,7},{7,5},{8,10},{10,8},{9,1... | collective-permute-start | bytes 786440 | tf_op jit(solution)/shard_map/ppermute | solution.py:31
  203.4 16.0 %collective-permute-start.40 = (bf16[64,2048]{1,0:T(8,128)(2,1)}, bf16[64,2048]{1,0:T(8,128)(2,1)}, u32[]{:S(2)}, u32[]{:S(2)}) collective-permute-start(bf16[64,2048]{1,0:T(8,128)(2,1)} %get-tuple-element.253), channel_id=1, source_target_pairs={{0,64},{64,0},{1,65},{65,1},{2,66},{66,2},{3,67},{67,3},{4,68},{68... | collective-permute-start | bytes 786440 | tf_op jit(solution)/shard_map/ppermute | solution.py:31
  204.9 14.5 %collective-permute-start.41 = (bf16[64,2048]{1,0:T(8,128)(2,1)}, bf16[64,2048]{1,0:T(8,128)(2,1)}, u32[]{:S(2)}, u32[]{:S(2)}) collective-permute-start(bf16[64,2048]{1,0:T(8,128)(2,1)} %get-tuple-element.252), channel_id=1, source_target_pairs={{0,66},{2,64},{64,2},{66,0},{1,67},{3,65},{65,3},{67,1},{4,70},{6,... | collective-permute-start | bytes 786440 | tf_op jit(solution)/shard_map/ppermute | solution.py:35
  219.4 168.1 %reduce-scatter.6.cloned.1.call-start = ((), (), s32[]{:S(2)}) async-start(), calls=%async_computation.6 | async-start | bytes 3932160 | tf_op jit(solution)/shard_map/reduce_scatter | solution.py:877
  223.7 13.1 %collective-permute-start.43 = (bf16[64,2048]{1,0:T(8,128)(2,1)S(1)}, bf16[64,2048]{1,0:T(8,128)(2,1)S(1)}, u32[]{:S(2)}, u32[]{:S(2)}) collective-permute-start(bf16[64,2048]{1,0:T(8,128)(2,1)S(1)} %get-tuple-element.220), channel_id=1, source_target_pairs={{0,64},{64,0},{1,65},{65,1},{2,66},{66,2},{3,67},{67,3},{4,68},{68... | collective-permute-start | bytes 786440 | tf_op jit(solution)/shard_map/ppermute | solution.py:31
  226.7 13.6 %collective-permute-start.44 = (bf16[64,2048]{1,0:T(8,128)(2,1)S(1)}, bf16[64,2048]{1,0:T(8,128)(2,1)S(1)}, u32[]{:S(2)}, u32[]{:S(2)}) collective-permute-start(bf16[64,2048]{1,0:T(8,128)(2,1)S(1)} %get-tuple-element.220), channel_id=1, source_target_pairs={{0,66},{2,64},{64,2},{66,0},{1,67},{3,65},{65,3},{67,1},{4,70},{6,... | collective-permute-start | bytes 786440 | tf_op jit(solution)/shard_map/ppermute | solution.py:35
  255.3 42.3 %collective-permute-start.46 = (bf16[2,512,128]{2,1,0:T(8,128)(2,1)}, bf16[2,512,128]{2,1,0:T(8,128)(2,1)S(1)}, u32[]{:S(2)}, u32[]{:S(2)}) collective-permute-start(bf16[2,512,128]{2,1,0:T(8,128)(2,1)} %get-tuple-element.155), channel_id=1, source_target_pairs={{0,4},{4,8},{8,12},{12,0},{1,5},{5,9},{9,13},{13,1},{2,6},{6,10},{... | collective-permute-start | bytes 786440 | tf_op jit(solution)/shard_map/ppermute | solution.py:61
  257.2 40.4 %collective-permute-start.47 = (bf16[2,512,128]{2,1,0:T(8,128)(2,1)}, bf16[2,512,128]{2,1,0:T(8,128)(2,1)S(1)}, u32[]{:S(2)}, u32[]{:S(2)}) collective-permute-start(bf16[2,512,128]{2,1,0:T(8,128)(2,1)} %get-tuple-element.156), channel_id=1, source_target_pairs={{0,12},{4,0},{8,4},{12,8},{1,13},{5,1},{9,5},{13,9},{2,14},{6,2},{... | collective-permute-start | bytes 786440 | tf_op jit(solution)/shard_map/ppermute | solution.py:61
  285.6 12.8 %collective-permute-start.48 = (bf16[2,512,128]{2,1,0:T(8,128)(2,1)}, bf16[2,512,128]{2,1,0:T(8,128)(2,1)S(1)}, u32[]{:S(2)}, u32[]{:S(2)}) collective-permute-start(bf16[2,512,128]{2,1,0:T(8,128)(2,1)} %get-tuple-element.157), channel_id=1, source_target_pairs={{0,16},{16,32},{32,48},{48,0},{1,17},{17,33},{33,49},{49,1},{2,18}... | collective-permute-start | bytes 786440 | tf_op jit(solution)/shard_map/ppermute | solution.py:61
  285.6 13.2 %collective-permute-start.49 = (bf16[2,512,128]{2,1,0:T(8,128)(2,1)}, bf16[2,512,128]{2,1,0:T(8,128)(2,1)S(1)}, u32[]{:S(2)}, u32[]{:S(2)}) collective-permute-start(bf16[2,512,128]{2,1,0:T(8,128)(2,1)} %get-tuple-element.158), channel_id=1, source_target_pairs={{0,48},{16,0},{32,16},{48,32},{1,49},{17,1},{33,17},{49,33},{2,50}... | collective-permute-start | bytes 786440 | tf_op jit(solution)/shard_map/ppermute | solution.py:61
  299.1 13.9 %collective-permute-start.50 = (bf16[4,512,128]{2,1,0:T(8,128)(2,1)S(1)}, bf16[4,512,128]{2,1,0:T(8,128)(2,1)S(1)}, u32[]{:S(2)}, u32[]{:S(2)}) collective-permute-start(bf16[4,512,128]{2,1,0:T(8,128)(2,1)S(1)} %get-tuple-element.167), channel_id=1, source_target_pairs={{0,4},{4,8},{8,12},{12,0},{1,5},{5,9},{9,13},{13,1},{2,6},{6,10},{... | collective-permute-start | bytes 1572872 | tf_op jit(solution)/shard_map/ppermute | solution.py:61
  299.2 15.0 %collective-permute-start.51 = (bf16[4,512,128]{2,1,0:T(8,128)(2,1)S(1)}, bf16[4,512,128]{2,1,0:T(8,128)(2,1)S(1)}, u32[]{:S(2)}, u32[]{:S(2)}) collective-permute-start(bf16[4,512,128]{2,1,0:T(8,128)(2,1)S(1)} %get-tuple-element.168), channel_id=1, source_target_pairs={{0,12},{4,0},{8,4},{12,8},{1,13},{5,1},{9,5},{13,9},{2,14},{6,2},{... | collective-permute-start | bytes 1572872 | tf_op jit(solution)/shard_map/ppermute | solution.py:61
  301.9 15.3 %collective-permute-start.52 = (bf16[4,512,128]{2,1,0:T(8,128)(2,1)S(1)}, bf16[4,512,128]{2,1,0:T(8,128)(2,1)S(1)}, u32[]{:S(2)}, u32[]{:S(2)}) collective-permute-start(bf16[4,512,128]{2,1,0:T(8,128)(2,1)S(1)} %get-tuple-element.169), channel_id=1, source_target_pairs={{0,16},{16,32},{32,48},{48,0},{1,17},{17,33},{33,49},{49,1},{2,18}... | collective-permute-start | bytes 1572872 | tf_op jit(solution)/shard_map/ppermute | solution.py:61
  301.9 16.5 %collective-permute-start.53 = (bf16[4,512,128]{2,1,0:T(8,128)(2,1)S(1)}, bf16[4,512,128]{2,1,0:T(8,128)(2,1)S(1)}, u32[]{:S(2)}, u32[]{:S(2)}) collective-permute-start(bf16[4,512,128]{2,1,0:T(8,128)(2,1)S(1)} %get-tuple-element.170), channel_id=1, source_target_pairs={{0,48},{16,0},{32,16},{48,32},{1,49},{17,1},{33,17},{49,33},{2,50}... | collective-permute-start | bytes 1572872 | tf_op jit(solution)/shard_map/ppermute | solution.py:61
  319.6 8.7 %collective-permute-start.57 = (bf16[512,128]{1,0:T(8,128)(2,1)S(1)}, bf16[512,128]{1,0:T(8,128)(2,1)S(1)}, u32[]{:S(2)}, u32[]{:S(2)}) collective-permute-start(bf16[512,128]{1,0:T(8,128)(2,1)S(1)} %get-tuple-element.274), channel_id=1, source_target_pairs={{0,4},{4,8},{8,12},{12,0},{1,5},{5,9},{9,13},{13,1},{2,6},{6,10},{... | collective-permute-start | bytes 393224 | tf_op jit(solution)/shard_map/ppermute | solution.py:61
  319.7 13.8 %collective-permute-start.58 = (bf16[512,128]{1,0:T(8,128)(2,1)S(1)}, bf16[512,128]{1,0:T(8,128)(2,1)S(1)}, u32[]{:S(2)}, u32[]{:S(2)}) collective-permute-start(bf16[512,128]{1,0:T(8,128)(2,1)S(1)} %get-tuple-element.273), channel_id=1, source_target_pairs={{0,8},{4,12},{8,0},{12,4},{1,9},{5,13},{9,1},{13,5},{2,10},{6,14},... | collective-permute-start | bytes 393224 | tf_op jit(solution)/shard_map/ppermute | solution.py:61
  320.2 13.3 %collective-permute-start.59 = (bf16[512,128]{1,0:T(8,128)(2,1)S(1)}, bf16[512,128]{1,0:T(8,128)(2,1)S(1)}, u32[]{:S(2)}, u32[]{:S(2)}) collective-permute-start(bf16[512,128]{1,0:T(8,128)(2,1)S(1)} %get-tuple-element.272), channel_id=1, source_target_pairs={{0,12},{4,0},{8,4},{12,8},{1,13},{5,1},{9,5},{13,9},{2,14},{6,2},{... | collective-permute-start | bytes 393224 | tf_op jit(solution)/shard_map/ppermute | solution.py:61
  322.6 11.0 %collective-permute-start.54 = (bf16[512,128]{1,0:T(8,128)(2,1)S(1)}, bf16[512,128]{1,0:T(8,128)(2,1)S(1)}, u32[]{:S(2)}, u32[]{:S(2)}) collective-permute-start(bf16[512,128]{1,0:T(8,128)(2,1)S(1)} %get-tuple-element.277), channel_id=1, source_target_pairs={{0,16},{16,32},{32,48},{48,0},{1,17},{17,33},{33,49},{49,1},{2,18}... | collective-permute-start | bytes 393224 | tf_op jit(solution)/shard_map/ppermute | solution.py:61
  322.7 10.9 %collective-permute-start.55 = (bf16[512,128]{1,0:T(8,128)(2,1)S(1)}, bf16[512,128]{1,0:T(8,128)(2,1)S(1)}, u32[]{:S(2)}, u32[]{:S(2)}) collective-permute-start(bf16[512,128]{1,0:T(8,128)(2,1)S(1)} %get-tuple-element.276), channel_id=1, source_target_pairs={{0,32},{16,48},{32,0},{48,16},{1,33},{17,49},{33,1},{49,17},{2,34}... | collective-permute-start | bytes 393224 | tf_op jit(solution)/shard_map/ppermute | solution.py:61
  338.8 9.9 %collective-permute-start.60 = (bf16[256,2048]{1,0:T(8,128)(2,1)S(1)}, bf16[256,2048]{1,0:T(8,128)(2,1)S(1)}, u32[]{:S(2)}, u32[]{:S(2)}) collective-permute-start(bf16[256,2048]{1,0:T(8,128)(2,1)S(1)} %add_convert_fusion), channel_id=1, source_target_pairs={{0,1},{1,0},{2,3},{3,2},{4,5},{5,4},{6,7},{7,6},{8,9},{9,8},{10,11... | collective-permute-start | bytes 3145736 | tf_op jit(solution)/shard_map/ppermute | solution.py:31
  354.1 10.4 %collective-permute-start.61 = (bf16[256,2048]{1,0:T(8,128)(2,1)}, bf16[256,2048]{1,0:T(8,128)(2,1)}, u32[]{:S(2)}, u32[]{:S(2)}) collective-permute-start(bf16[256,2048]{1,0:T(8,128)(2,1)} %convolution_convert_fusion.1), channel_id=1, source_target_pairs={{0,1},{1,0},{2,3},{3,2},{4,5},{5,4},{6,7},{7,6},{8,9},{9,8},{10,11... | collective-permute-start | bytes 3145736 | tf_op jit(solution)/shard_map/ppermute | solution.py:31
  355.4 51.0 %all-to-all-start = ((bf16[16,144,256]{2,1,0:T(8,128)(2,1)}), bf16[16,144,256]{2,1,0:T(8,128)(2,1)}, u32[]{:S(2)}, u32[]{:S(2)}) async-start(bf16[16,144,256]{2,1,0:T(8,128)(2,1)} %plane_grads.5), calls=%async_computation | async-start | bytes 2359296 | tf_op jit(solution)/shard_map/all_to_all | solution.py:893
  360.3 52.3 %reduce-scatter.8.cloned.1.call-start = ((), (), s32[]{:S(2)}) async-start(), calls=%async_computation.7 | async-start | bytes 983040 | tf_op jit(solution)/shard_map/reduce_scatter | solution.py:880
  360.6 11.0 %collective-permute-start.66 = (bf16[64,2048]{1,0:T(8,128)(2,1)S(1)}, bf16[64,2048]{1,0:T(8,128)(2,1)S(1)}, u32[]{:S(2)}, u32[]{:S(2)}) collective-permute-start(bf16[64,2048]{1,0:T(8,128)(2,1)S(1)} %get-tuple-element.243), channel_id=1, source_target_pairs={{0,2},{2,0},{1,3},{3,1},{4,6},{6,4},{5,7},{7,5},{8,10},{10,8},{9,1... | collective-permute-start | bytes 786440 | tf_op jit(solution)/shard_map/ppermute | solution.py:31
  360.7 13.7 %collective-permute-start.67 = (bf16[64,2048]{1,0:T(8,128)(2,1)S(1)}, bf16[64,2048]{1,0:T(8,128)(2,1)S(1)}, u32[]{:S(2)}, u32[]{:S(2)}) collective-permute-start(bf16[64,2048]{1,0:T(8,128)(2,1)S(1)} %get-tuple-element.245), channel_id=1, source_target_pairs={{0,64},{64,0},{1,65},{65,1},{2,66},{66,2},{3,67},{67,3},{4,68},{68... | collective-permute-start | bytes 786440 | tf_op jit(solution)/shard_map/ppermute | solution.py:31
  362.4 14.0 %collective-permute-start.68 = (bf16[64,2048]{1,0:T(8,128)(2,1)S(1)}, bf16[64,2048]{1,0:T(8,128)(2,1)S(1)}, u32[]{:S(2)}, u32[]{:S(2)}) collective-permute-start(bf16[64,2048]{1,0:T(8,128)(2,1)S(1)} %get-tuple-element.244), channel_id=1, source_target_pairs={{0,66},{2,64},{64,2},{66,0},{1,67},{3,65},{65,3},{67,1},{4,70},{6,... | collective-permute-start | bytes 786440 | tf_op jit(solution)/shard_map/ppermute | solution.py:35
  369.9 17.7 %collective-permute-start.62 = (bf16[64,2048]{1,0:T(8,128)(2,1)}, bf16[64,2048]{1,0:T(8,128)(2,1)}, u32[]{:S(2)}, u32[]{:S(2)}) collective-permute-start(bf16[64,2048]{1,0:T(8,128)(2,1)} %get-tuple-element.247), channel_id=1, source_target_pairs={{0,2},{2,0},{1,3},{3,1},{4,6},{6,4},{5,7},{7,5},{8,10},{10,8},{9,1... | collective-permute-start | bytes 786440 | tf_op jit(solution)/shard_map/ppermute | solution.py:31
  369.9 17.7 %collective-permute-start.63 = (bf16[64,2048]{1,0:T(8,128)(2,1)}, bf16[64,2048]{1,0:T(8,128)(2,1)}, u32[]{:S(2)}, u32[]{:S(2)}) collective-permute-start(bf16[64,2048]{1,0:T(8,128)(2,1)} %get-tuple-element.249), channel_id=1, source_target_pairs={{0,64},{64,0},{1,65},{65,1},{2,66},{66,2},{3,67},{67,3},{4,68},{68... | collective-permute-start | bytes 786440 | tf_op jit(solution)/shard_map/ppermute | solution.py:31
  371.6 16.0 %collective-permute-start.64 = (bf16[64,2048]{1,0:T(8,128)(2,1)S(1)}, bf16[64,2048]{1,0:T(8,128)(2,1)}, u32[]{:S(2)}, u32[]{:S(2)}) collective-permute-start(bf16[64,2048]{1,0:T(8,128)(2,1)S(1)} %get-tuple-element.248), channel_id=1, source_target_pairs={{0,66},{2,64},{64,2},{66,0},{1,67},{3,65},{65,3},{67,1},{4,70},{6,... | collective-permute-start | bytes 786440 | tf_op jit(solution)/shard_map/ppermute | solution.py:35
  389.1 9.0 %collective-permute-start.65 = (bf16[64,2048]{1,0:T(8,128)(2,1)S(1)}, bf16[64,2048]{1,0:T(8,128)(2,1)S(1)}, u32[]{:S(2)}, u32[]{:S(2)}) collective-permute-start(bf16[64,2048]{1,0:T(8,128)(2,1)S(1)} %fusion.42), channel_id=1, source_target_pairs={{0,2},{2,0},{1,3},{3,1},{4,6},{6,4},{5,7},{7,5},{8,10},{10,8},{9,1... | collective-permute-start | bytes 786440 | tf_op jit(solution)/shard_map/ppermute | solution.py:31
  393.2 13.2 %collective-permute-start.69 = (bf16[64,2304]{1,0:T(8,128)(2,1)S(1)}, bf16[64,2304]{1,0:T(8,128)(2,1)S(1)}, u32[]{:S(2)}, u32[]{:S(2)}) collective-permute-start(bf16[64,2304]{1,0:T(8,128)(2,1)S(1)} %get-tuple-element.197), channel_id=1, source_target_pairs={{0,64},{64,0},{1,65},{65,1},{2,66},{66,2},{3,67},{67,3},{4,68},{68... | collective-permute-start | bytes 884744 | tf_op jit(solution)/shard_map/ppermute | solution.py:31
  417.6 9.2 %collective-permute-start.73 = (bf16[64,1152]{1,0:T(8,128)(2,1)S(1)}, bf16[64,1152]{1,0:T(8,128)(2,1)S(1)}, u32[]{:S(2)}, u32[]{:S(2)}) collective-permute-start(bf16[64,1152]{1,0:T(8,128)(2,1)S(1)} %fusion.64), channel_id=1, source_target_pairs={{0,64},{64,0},{1,65},{65,1},{2,66},{66,2},{3,67},{67,3},{4,68},{68... | collective-permute-start | bytes 442376 | tf_op jit(solution)/shard_map/ppermute | solution.py:31
  421.6 12.1 %collective-permute-start.71 = (bf16[64,2048]{1,0:T(8,128)(2,1)S(1)}, bf16[64,2048]{1,0:T(8,128)(2,1)S(1)}, u32[]{:S(2)}, u32[]{:S(2)}) collective-permute-start(bf16[64,2048]{1,0:T(8,128)(2,1)S(1)} %reduce-precision_convert_fusion), channel_id=1, source_target_pairs={{0,2},{2,0},{1,3},{3,1},{4,6},{6,4},{5,7},{7,5},{8,10},{10,8},{9,1... | collective-permute-start | bytes 786440 | tf_op jit(solution)/shard_map/ppermute | solution.py:31
  422.1 12.1 %collective-permute-start.70 = (bf16[128,2048]{1,0:T(8,128)(2,1)}, bf16[128,2048]{1,0:T(8,128)(2,1)S(1)}, u32[]{:S(2)}, u32[]{:S(2)}) collective-permute-start(bf16[128,2048]{1,0:T(8,128)(2,1)} %pad_maximum_fusion.9), channel_id=1, source_target_pairs={{0,1},{1,0},{2,3},{3,2},{4,5},{5,4},{6,7},{7,6},{8,9},{9,8},{10,11... | collective-permute-start | bytes 1572872 | tf_op jit(solution)/shard_map/ppermute | solution.py:31
  (89 other events, 865.8 us)
Sparse Core Ops, SparseCore 0:
  23.5 55.5 all-gather.2
  81.2 87.7 all-gather.4
  219.6 109.0 reduce-scatter.9
  334.6 52.9 reduce-scatter.5
  389.9 22.6 reduce-scatter.7
